TPU v7x, 32 devices: a whole 2x2x4 slice. The times are simulated.
32 devices in a mesh: dp: 8 (over z, x), fsdp: 4 (over y, core).
Axes of the slice: x: 2, y: 2, z: 4, core: 2. Of those that a mesh axis runs over, the one named last changes fastest.
Arguments:
- tokens: bfloat16 [262144, 128], P(('dp', 'fsdp')), may hold values from -6 to 6
- points: bfloat16 [64, 3, 1024, 128], P(('dp', 'fsdp')), may hold values from -6 to 6
- coords: float32 [2, 262144], P(None, ('dp', 'fsdp')), may hold values from -1 to 1
- presence: int32 [64, 3], P(('dp', 'fsdp')), may hold values from 0 to 1, as said below
- counts: int32 [64, 3], P(('dp', 'fsdp')), may hold values from 256 to 1024, as said below
- cotangent: bfloat16 [262144, 128], P(('dp', 'fsdp')), may hold values from -6 to 6
- gain_first: bfloat16 [128], P('fsdp'), may hold values from 0.5 to 1.5
- bias_first: bfloat16 [128], P('fsdp'), may hold values from -2.5 to 2.5
- query_first: bfloat16 [128, 128], P('fsdp'), may hold values from -0.5 to 0.5
- key_first: bfloat16 [128, 128], P('fsdp'), may hold values from -0.5 to 0.5
- value_first: bfloat16 [128, 128], P('fsdp'), may hold values from -0.5 to 0.5
- out_first: bfloat16 [128, 128], P('fsdp'), may hold values from -6 to 6
- query_second: bfloat16 [128, 128], P('fsdp'), may hold values from -0.5 to 0.5
- key_second: bfloat16 [128, 128], P('fsdp'), may hold values from -0.5 to 0.5
- value_second: bfloat16 [128, 128], P('fsdp'), may hold values from -0.5 to 0.5
- out_second: bfloat16 [128, 128], P('fsdp'), may hold values from -6 to 6
- gain_second: bfloat16 [128], P('fsdp'), may hold values from 0.5 to 1.5
- bias_second: bfloat16 [128], P('fsdp'), may hold values from -2.5 to 2.5
- expert_in: bfloat16 [4, 128, 256], P(None, 'fsdp'), may hold values from -0.5 to 0.5
- expert_out: bfloat16 [4, 256, 128], P(None, 'fsdp'), may hold values from -0.375 to 0.375
- gate_weight: bfloat16 [2, 4], P(None, 'fsdp'), may hold values from -3 to 3
Outputs:
- result: bfloat16 [262144, 128], P(('dp', 'fsdp'))
- grad_tokens: float32 [262144, 128], P(('dp', 'fsdp'))
- grad_gain_first: float32 [128], P('fsdp')
- grad_bias_first: float32 [128], P('fsdp')
- grad_query_first: float32 [128, 128], P('fsdp')
- grad_key_first: float32 [128, 128], P('fsdp')
- grad_value_first: float32 [128, 128], P('fsdp')
- grad_out_first: float32 [128, 128], P('fsdp')
- grad_query_second: float32 [128, 128], P('fsdp')
- grad_key_second: float32 [128, 128], P('fsdp')
- grad_value_second: float32 [128, 128], P('fsdp')
- grad_out_second: float32 [128, 128], P('fsdp')
- grad_gain_second: float32 [128], P('fsdp')
- grad_bias_second: float32 [128], P('fsdp')
- grad_expert_in: float32 [4, 128, 256], P(None, 'fsdp')
- grad_expert_out: float32 [4, 256, 128], P(None, 'fsdp')
- grad_gate_weight: float32 [2, 4], P(None, 'fsdp')
Inputs may be any that keep to these rules, and one draw needn't show every extreme that they name: `presence`: each item has at least one of its 3 input functions present. `counts`: slots of an input function from its count on are padding; the count 1024 occurs in every draw.
All inputs are finite; a program needn't handle non-finite values.
Results may differ from a plain program's by a relative error of at most 0.029.
Values may be sent and summed in bfloat16 or wider, within the bound.
No kernel may reach another device: no remote copies, remote signals or barrier semaphores. Data moves between devices by JAX's collectives and lax.ppermute only.
A program may use at most 256 MiB of HBM per device.

v0:
```python
from functools import partial

import jax
import jax.numpy as jnp
from jax import lax
from jax.experimental import pallas as pl
from jax.experimental.pallas import tpu as pltpu
from jax.sharding import PartitionSpec as P


HEADS = 8
eps = 1e-05
f32 = jnp.float32
bf16 = jnp.bfloat16
MAIN_TILE = 4096
REST_TILE = 1024
GROUP = 1024
STRIP = 128
CHUNK = 256
SLAB = 64
PAD = 16
VMEM = 60 * 1024 * 1024


def cost(microseconds):
    return pl.CostEstimate(flops=microseconds * 10**9, bytes_accessed=10**6, transcendentals=0)


def nn(left, right):
    return jnp.dot(left, right, preferred_element_type=f32)


def nt(left, right):
    return lax.dot_general(left, right, (((1,), (1,)), ((), ())), preferred_element_type=f32)


def flip(value):
    return value.T


def inverse(value):
    return pl.reciprocal(value, approx=True)


def head_softmax(value):
    width, rows = value.shape
    split = value.reshape(HEADS, width // HEADS, rows)
    raised = jnp.exp(split - jnp.max(split, axis=1, keepdims=True))
    return (raised * inverse(jnp.sum(raised, axis=1, keepdims=True))).reshape(width, rows)


def softmax_back(probs, grad):
    width, rows = grad.shape
    probs = probs.astype(f32).reshape(HEADS, width // HEADS, rows)
    grad = grad.reshape(HEADS, width // HEADS, rows)
    inner = jnp.sum(probs * grad, axis=1, keepdims=True)
    return (probs * (grad - inner)).reshape(width, rows)


def standardize(value):
    centre = value - jnp.mean(value, axis=0, keepdims=True)
    scale = lax.rsqrt(jnp.mean(centre * centre, axis=0, keepdims=True) + eps)
    return centre * scale, scale


def norm_back(grad, hat, scale):
    return scale * (
        grad
        - jnp.mean(grad, axis=0, keepdims=True)
        - hat * jnp.mean(grad * hat, axis=0, keepdims=True)
    )


def same_head(width):
    shape, head = (width, width), width // HEADS
    row = lax.broadcasted_iota(jnp.int32, shape, 0)
    column = lax.broadcasted_iota(jnp.int32, shape, 1)
    return lax.div(row, head) == lax.div(column, head)


def own_head(width):
    shape, head = (HEADS, width), width // HEADS
    row = lax.broadcasted_iota(jnp.int32, shape, 0)
    return row == lax.div(lax.broadcasted_iota(jnp.int32, shape, 1), head)


def by_head(value, scales):
    width, rows = value.shape
    split = value.reshape(HEADS, width // HEADS, rows)
    return (split * scales.reshape(HEADS, 1, rows)).reshape(width, rows)


def head_sums(value):
    width, rows = value.shape
    return jnp.sum(value.reshape(HEADS, width // HEADS, rows), axis=1)


def totals_column(rows, width):
    row = jnp.sum(jnp.where(own_head(width), rows, 0.0), axis=0, keepdims=True)
    return flip(jnp.broadcast_to(-row, (width, width)))


def pack_states(lefts, totals, state_t, state, width):
    count = len(lefts)
    rights = [jnp.where(own_head(width), total, 0.0) for total in totals]
    rest = jnp.zeros((width - count * HEADS, width), f32)
    right = jnp.concatenate(rights + [rest], axis=0)
    for place, left in enumerate(lefts):
        span = slice(place * width, (place + 1) * width)
        state_t[span] = left.astype(bf16)
        state[:, span] = flip(left).astype(bf16)
    start = count * width
    used = state_t.shape[0] - start
    state_t[start:] = right[:used].astype(bf16)
    state[:, start : start + width] = -flip(right).astype(bf16)


def assemble(parts, gathered):
    shards = len(parts)
    here = lax.axis_index("fsdp")
    for place, part in enumerate(parts):
        gathered[lax.rem(here + shards - place, shards)] = part[...]


def columns(gathered, start, count):
    shards, _, width = gathered.shape
    piece = width // shards
    small = [gathered[shard, start : start + 16, :].astype(f32) for shard in range(shards)]
    joined = jnp.concatenate([part[:, :piece] for part in small], axis=1)
    return [
        flip(jnp.broadcast_to(joined[place : place + 1], (width, width)))[:, 0:1]
        for place in range(count)
    ]


def lane_fold(value):
    width = value.shape[0]
    total = value[:, :width]
    for start in range(width, value.shape[1], width):
        total = total + value[:, start : start + width]
    return total


def as_row(value):
    width = value.shape[0]
    return flip(jnp.broadcast_to(jnp.sum(value, axis=1, keepdims=True), (width, width)))


def scatter_blocks(stage, outs):
    shards = len(outs)
    here = lax.axis_index("fsdp")
    for place, out in enumerate(outs):
        out[...] = stage[lax.rem(here + place, shards)]


def whole(gathered, start, rows):
    shards = gathered.shape[0]
    return gathered[:, start : start + rows, :].reshape(shards * rows, gathered.shape[2])


def function_weight(presence, item, func, funcs, shape):
    total = presence[item, 0]
    for other in range(1, funcs):
        total = total + presence[item, other]
    own = jnp.full(shape, presence[item, func], jnp.int32).astype(f32)
    return own / jnp.full(shape, total, jnp.int32).astype(f32)


def pack_kernel(*refs):
    weights, vectors, gate = refs[:10], refs[10:14], refs[14]
    early, late = refs[15:]
    keys, values, query, out, query_two, key_two, value_two, out_two, enter, leave = weights
    start = 0
    for weight in (keys, values):
        early[start : start + weight.shape[0]] = weight[...]
        start += weight.shape[0]
    start = 0
    for weight in (query, out, query_two, key_two, value_two, out_two):
        late[start : start + weight.shape[0]] = weight[...]
        start += weight.shape[0]
    experts, piece, hidden = enter.shape
    width = late.shape[1]
    for expert in range(experts):
        for half in range(hidden // width):
            late[start : start + piece] = enter[expert, :, half * width : (half + 1) * width]
            start += piece
    for expert in range(experts):
        late[start : start + leave.shape[1]] = leave[expert]
        start += leave.shape[1]
    rest = jnp.zeros((1, width - piece), f32)
    rows = [
        jnp.concatenate([vector[...].astype(f32), rest], axis=1) for vector in vectors
    ]
    rows.append(jnp.zeros((4, width), f32))
    for row in range(2):
        rows.append(jnp.broadcast_to(gate[row : row + 1, 0:1].astype(f32), (1, width)))
    rows.append(jnp.zeros((6, width), f32))
    late[start : start + 16] = jnp.concatenate(rows, axis=0).astype(bf16)


def run_tasks(tasks):
    waiting = None
    for dots, work in tasks:
        found = dots()
        if waiting is not None:
            waiting[0](*waiting[1])
        waiting = (work, found)
    waiting[0](*waiting[1])


def mix(tasks, extra):
    mixed = []
    done = 0
    for place, task in enumerate(tasks, 1):
        mixed.append(task)
        due = len(extra) * place // len(tasks)
        mixed += extra[done:due]
        done = due
    return mixed


def behind(stage, total, chunks, groups):
    tasks = []
    for cols in chunks:
        tasks.append(stage(cols))
        tasks += [total(group) for group in groups if group.stop == cols.stop - 2 * CHUNK]
    return tasks


def add_to(ref, span):
    def work(value):
        ref[span] += value

    return work


def points_forward(counts, presence, points, *refs, funcs, shards):
    parts = refs[:shards]
    state_t, state, keys_out, values_out, gathered, weight = refs[shards:]
    item = pl.program_id(0)
    width = points.shape[2]
    slots = points.shape[1]
    piece = width // shards

    @pl.when(item == 0)
    def _():
        assemble(parts, gathered)
        weight[:width] = flip(whole(gathered, 0, piece))
        weight[width:] = flip(whole(gathered, piece, piece))

    chunks = [slice(start, start + CHUNK) for start in range(0, slots, CHUNK)]

    def project(func, cols):
        def dots():
            return (nt(weight[...], points[func, cols, :]),)

        def work(both):
            slot = cols.start + lax.broadcasted_iota(jnp.int32, (1, CHUNK), 1)
            probs = head_softmax(both[:width])
            keys = jnp.where(slot < counts[item, func], probs, 0.0)
            keys_out[func, :, cols] = keys.astype(bf16)
            values_out[func, :, cols] = both[width:].astype(bf16)

        return dots, work

    def summarize(func):
        values = values_out[func]
        extended = jnp.concatenate([values, jnp.ones((PAD, slots), bf16)], axis=0)
        share = function_weight(presence, item, func, funcs, (1, width))
        summed = nt(extended, keys_out[func])
        left = jnp.where(same_head(width), summed[:width], 0.0) * share
        return left, summed[width : width + 1]

    run_tasks([project(func, cols) for func in range(funcs) for cols in chunks])
    lefts, totals = zip(*(summarize(func) for func in range(funcs)))
    pack_states(lefts, totals, state_t.at[0], state.at[0], width)


def main_kernel(tokens, cotangent, coords, state_t, *refs, funcs, experts, shards, at):
    parts, outs, scratch = refs[:shards], refs[shards : 2 * shards + 14], refs[2 * shards + 14 :]
    (
        result,
        queries_out,
        cross_out,
        first_out,
        keys_out,
        values_out,
        grad_q_out,
        grad_second_out,
        grad_state_out,
        rest_weights,
        rest_vectors,
        normed_out,
        hat_out,
        scale_out,
    ) = outs[:14]
    grads_out = outs[14:]
    (
        params,
        grads_stage,
        first_keep,
        query_keep,
        state_sum,
        self_t,
        self_state,
        grad_state_sum,
        w_query,
        w_out_one,
        w_self,
        w_out_two_t,
        w_out_two,
        w_in_t,
        w_in,
        w_exit,
        w_exit_t,
        gain_one,
        bias_one,
        gain_two,
        bias_two,
        hidden_keep,
        inner_keep,
        normed_keep,
        grad_keep,
        own_keep,
        pair_keep,
        sum_in,
        sum_exit,
        sum_out_two,
        sum_gain,
        sum_bias,
        sum_gate,
    ) = scratch
    item = pl.program_id(0)
    phase = pl.program_id(1)
    step = pl.program_id(2)
    steps = pl.num_programs(2)
    width = tokens.shape[1]
    rows = tokens.shape[0]
    piece = width // shards
    hidden = w_in.shape[1] // experts
    exit_piece = hidden // shards

    @pl.when((item == 0) & (phase == 0) & (step == 0))
    def _():
        assemble(parts, params)
        w_query[...] = flip(whole(params, at["query_first"], piece))
        w_out_one[...] = flip(whole(params, at["out_first"], piece))
        w_self[:width] = flip(whole(params, at["query_second"], piece))
        w_self[width : 2 * width] = flip(whole(params, at["key_second"], piece))
        w_self[2 * width :] = flip(whole(params, at["value_second"], piece))
        out_two = whole(params, at["out_second"], piece)
        w_out_two[...] = out_two
        w_out_two_t[...] = flip(out_two)
        for block in range(experts * hidden // width):
            part = whole(params, at["expert_in"] + block * piece, piece)
            w_in[:, block * width : (block + 1) * width] = part
            w_in_t[block * width : (block + 1) * width] = flip(part)
        for expert in range(experts):
            part = whole(params, at["expert_out"] + expert * exit_piece, exit_piece)
            w_exit[expert * hidden : (expert + 1) * hidden] = part
            w_exit_t[:, expert * hidden : (expert + 1) * hidden] = flip(part)
        names = ("query_second", "key_second", "value_second", "out_first", "query_first")
        for place, name in enumerate(names):
            rest_weights[:, place * width : (place + 1) * width] = whole(params, at[name], piece)
        found = columns(params, at["small"], 4)
        rest_vectors[...] = jnp.broadcast_to(found[0], rest_vectors.shape)
        for vector, column in zip((gain_one, bias_one, gain_two, bias_two), found):
            vector[...] = jnp.broadcast_to(column, vector.shape)
        sum_in[...] = jnp.zeros_like(sum_in)
        sum_exit[...] = jnp.zeros_like(sum_exit)
        sum_out_two[...] = jnp.zeros_like(sum_out_two)
        sum_gain[...] = jnp.zeros_like(sum_gain)
        sum_bias[...] = jnp.zeros_like(sum_bias)
        sum_gate[...] = jnp.zeros_like(sum_gate)

    chunks = [slice(start, start + CHUNK) for start in range(0, rows, CHUNK)]
    groups = [slice(start, start + GROUP) for start in range(0, rows, GROUP)]
    every = slice(None)

    @pl.when((phase == 0) & (step == 0))
    def _():
        state_sum[...] = jnp.zeros_like(state_sum)
        grad_state_sum[...] = jnp.zeros_like(grad_state_sum)

    @pl.when(phase == 0)
    def _():
        def enter(cols):
            def dots():
                return (flip(tokens[cols, :]).astype(f32),)

            def work(rows_t):
                first_keep[step, :, cols] = rows_t
                hat, scale = standardize(rows_t)
                hat_out[:, cols] = hat.astype(bf16)
                scale_out[:, cols] = jnp.broadcast_to(scale, (8, CHUNK))
                normed_out[:, cols] = (hat * gain_one[...] + bias_one[...]).astype(bf16)

            return dots, work

        def ask(cols):
            def dots():
                return (nn(w_query[...], normed_out[:, cols]),)

            def work(value):
                queries_out[:, cols] = head_softmax(value).astype(bf16)

            return dots, work

        def across(cols):
            def dots():
                return (nn(state_t[0], queries_out[:, cols]),)

            def work(both):
                undo = inverse(both[funcs * width :])
                mixed = None
                for func in range(funcs):
                    part = by_head(
                        both[func * width : (func + 1) * width],
                        undo[func * HEADS : (func + 1) * HEADS],
                    )
                    mixed = part if mixed is None else mixed + part
                cross_out[:, cols] = mixed.astype(bf16)

            return dots, work

        def leave(cols):
            def dots():
                return (nn(w_out_one[...], cross_out[:, cols]),)

            def work(value):
                first = first_keep[step, :, cols] + value
                first_keep[step, :, cols] = first
                first_out[:, cols] = first.astype(bf16)

            return dots, work

        def project(cols):
            def dots():
                return (nn(w_self[...], first_out[:, cols]),)

            def work(three):
                query_keep[step, :, cols] = head_softmax(three[:width]).astype(bf16)
                keys_out[:, cols] = head_softmax(three[width : 2 * width]).astype(bf16)
                values = three[2 * width :].astype(bf16)
                values_out[:, cols] = values
                pair_keep[:width, cols] = values
                pair_keep[width:, cols] = jnp.ones((PAD, CHUNK), bf16)

            return dots, work

        def sum_state(cols):
            return (
                lambda: (nt(pair_keep[:, cols], keys_out[:, cols]),),
                add_to(state_sum, every),
            )

        tasks = [stage(cols) for stage in (enter, ask, across, leave) for cols in chunks]
        run_tasks(tasks + behind(project, sum_state, chunks, groups[:-1]))
        run_tasks([sum_state(groups[-1])])

        @pl.when(step == steps - 1)
        def _():
            left = jnp.where(same_head(width), state_sum[:width], 0.0)
            pack_states([left], [state_sum[width : width + 1]], self_t, self_state, width)

    @pl.when(phase == 1)
    def _():
        undo_of, norm_of, gates_of = {}, {}, {}
        grad_gates_of = {chunk.start: [] for chunk in chunks}

        def attend(cols):
            def dots():
                return (nn(self_t[...], query_keep[step, :, cols]),)

            def work(both):
                undo = inverse(both[width : width + HEADS])
                undo_of[cols.start] = undo
                own_keep[:, cols] = by_head(both[:width], undo).astype(bf16)
                grad_keep[:, cols] = flip(cotangent[cols, :])

            return dots, work

        def gate(cols):
            across, down = coords[0:1, cols], coords[1:2, cols]
            logits = []
            for expert in range(experts):
                pair = params[expert, at["small"] : at["small"] + 16, 0:1].astype(f32)
                logits.append(across * pair[8:9] + down * pair[9:10])
            peak = logits[0]
            for logit in logits[1:]:
                peak = jnp.maximum(peak, logit)
            raised = [jnp.exp(logit - peak) for logit in logits]
            total = raised[0]
            for other in raised[1:]:
                total = total + other
            return [other / total for other in raised]

        def norm(cols):
            def dots():
                return (nn(w_out_two_t[...], own_keep[:, cols]),)

            def work(value):
                second = first_keep[step, :, cols] + value
                first_keep[step, :, cols] = second
                hat, scale = standardize(second)
                norm_of[cols.start] = (hat, scale)
                normed_keep[:, cols] = (hat * gain_two[...] + bias_two[...]).astype(bf16)
                gates_of[cols.start] = gate(cols)

            return dots, work

        def ring(cols):
            start = cols.start % (2 * GROUP)
            return slice(start, start + cols.stop - cols.start)

        def expand(cols, first):
            expert = first // hidden
            strip = slice(first, first + STRIP)

            def dots():
                return (
                    nn(w_in_t[strip], normed_keep[:, cols]).astype(bf16),
                    nn(w_exit[strip], grad_keep[:, cols]).astype(bf16),
                )

            def work(inners, backs):
                share = (0.5 * gates_of[cols.start][expert]).astype(bf16)
                partial_sum = None
                for start in range(0, STRIP, SLAB):
                    inner, back = inners[start : start + SLAB], backs[start : start + SLAB]
                    span = slice(first + start, first + start + SLAB)
                    square = inner * inner
                    tanh = jnp.tanh(inner * (0.7978845608028654 + 0.035677408136300125 * square))
                    above = 1.0 + tanh
                    active = inner * above
                    product = active * back
                    folded = product[:16]
                    for row in range(16, SLAB, 16):
                        folded = folded + product[row : row + 16]
                    folded = folded.astype(f32)
                    partial_sum = folded if partial_sum is None else partial_sum + folded
                    hidden_keep[span, ring(cols)] = active * share
                    slope = above + active * (1.0 - tanh) * (
                        0.7978845608028654 + 0.10703222440890037 * square
                    )
                    inner_keep[span, ring(cols)] = slope * (back * share)
                found = jnp.sum(0.5 * partial_sum, axis=0, keepdims=True)
                if first % hidden:
                    grad_gates_of[cols.start][expert] += found
                else:
                    grad_gates_of[cols.start].append(found)

            return dots, work

        def contract(cols):
            def dots():
                return (
                    nn(w_exit_t[...], hidden_keep[:, ring(cols)]),
                    nn(w_in[...], inner_keep[:, ring(cols)]),
                )

            def work(mixed, grad_normed):
                result[cols, :] = flip((first_keep[step, :, cols] + mixed).astype(bf16))
                hat, scale = norm_of[cols.start]
                sum_gain[...] += lane_fold(grad_normed * hat)
                sum_bias[...] += lane_fold(grad_normed)
                grad_second = grad_keep[:, cols].astype(f32) + norm_back(
                    grad_normed * gain_two[...], hat, scale
                )
                grad_second_out[:, cols] = grad_second.astype(bf16)
                gates, grad_gates = gates_of[cols.start], grad_gates_of[cols.start]
                across, down = coords[0:1, cols], coords[1:2, cols]
                mean_gate = gates[0] * grad_gates[0]
                for expert in range(1, experts):
                    mean_gate = mean_gate + gates[expert] * grad_gates[expert]
                for expert in range(experts):
                    change = gates[expert] * (grad_gates[expert] - mean_gate)
                    sum_gate[expert : expert + 1, cols] += across * change
                    sum_gate[experts + expert : experts + expert + 1, cols] += down * change

            return dots, work

        def attend_back(cols):
            def dots():
                return (nn(w_out_two[...], grad_second_out[:, cols]),)

            def work(value):
                share = by_head(value, undo_of[cols.start])
                pair_keep[:width, cols] = share.astype(bf16)
                sums = head_sums(share * own_keep[:, cols].astype(f32))
                pair_keep[width:, cols] = jnp.concatenate(
                    [sums, jnp.zeros((PAD - HEADS, CHUNK), f32)], axis=0
                ).astype(bf16)

            return dots, work

        def query_back(cols):
            def dots():
                return (nn(self_state[:, : width + PAD], pair_keep[:, cols]),)

            def work(grad_q):
                queries = query_keep[step, :, cols]
                grad_q_out[:, cols] = softmax_back(queries, grad_q).astype(bf16)

            return dots, work

        def sum_hidden(cols, expert):
            span = slice(expert * hidden, (expert + 1) * hidden)
            return (
                lambda: (nn(hidden_keep[span, ring(cols)], cotangent[cols, :]),),
                add_to(sum_exit, span),
            )

        def sum_inner(cols, expert):
            span = slice(expert * hidden, (expert + 1) * hidden)
            return (
                lambda: (nt(inner_keep[span, ring(cols)], normed_keep[:, cols]),),
                add_to(sum_in, span),
            )

        def sum_own(cols):
            return (
                lambda: (nt(own_keep[:, cols], grad_second_out[:, cols]),),
                add_to(sum_out_two, every),
            )

        def sum_pair(cols):
            return (
                lambda: (nt(pair_keep[:, cols], query_keep[step, :, cols]),),
                add_to(grad_state_sum, every),
            )

        tasks = [stage(cols) for stage in (attend, norm) for cols in chunks]
        sums, contracts = [], []
        for group in groups:
            inside = [cols for cols in chunks if group.start <= cols.start < group.stop]
            expands = [
                expand(cols, first) for cols in inside for first in range(0, experts * hidden, STRIP)
            ]
            tasks += mix(expands, mix(sums, contracts) if sums else [])
            contracts = [contract(cols) for cols in inside]
            sums = [
                total(group, expert) for expert in range(experts) for total in (sum_hidden, sum_inner)
            ]
        tasks += mix(contracts + [attend_back(cols) for cols in chunks], sums)
        last = [total(group) for group in groups for total in (sum_own, sum_pair)]
        tasks += mix([query_back(cols) for cols in chunks], last)
        run_tasks(tasks)

        @pl.when(step == steps - 1)
        def _():
            grad_state_out[0] = grad_state_sum[...]

    @pl.when((item == pl.num_programs(0) - 1) & (phase == 1) & (step == steps - 1))
    def _():
        gain, bias = as_row(sum_gain[...]), as_row(sum_bias[...])
        gate = jnp.broadcast_to(jnp.sum(sum_gate[...], axis=1, keepdims=True), (8, width))
        row = lax.broadcasted_iota(jnp.int32, (8, width), 0)
        vectors = jnp.where(row == 0, gain[:8], bias[:8])
        small = jnp.concatenate([vectors, gate], axis=0).astype(bf16)
        start = 0
        for block in range(experts * hidden // width):
            part = flip(sum_in[block * width : (block + 1) * width]).astype(bf16)
            grads_stage[:, start : start + piece, :] = part.reshape(shards, piece, width)
            start += piece
        for expert in range(experts):
            part = sum_exit[expert * hidden : (expert + 1) * hidden].astype(bf16)
            grads_stage[:, start : start + exit_piece, :] = part.reshape(shards, exit_piece, width)
            start += exit_piece
        part = sum_out_two[...].astype(bf16)
        grads_stage[:, start : start + piece, :] = part.reshape(shards, piece, width)
        start += piece
        for shard in range(shards):
            grads_stage[shard, start : start + 16, :] = small
        scatter_blocks(grads_stage, grads_out)


def rest_kernel(
    presence,
    hat_in,
    scale_in,
    normed_in,
    queries_in,
    cross_in,
    first_in,
    keys_in,
    values_in,
    grad_q_in,
    grad_second_in,
    grad_state_in,
    state_t,
    state,
    weights,
    gain_one,
    *refs,
    funcs,
    item,
    first_call,
):
    if not first_call:
        carry, refs = refs[3], refs[5:]
    (
        grad_tokens,
        grad_cross_state_out,
        grad_totals_out,
        sums_out,
        grad_self_state,
        grad_totals,
        grad_state_sum,
        sums,
        three_keep,
        cross_keep,
        stack_keep,
        query_keep,
    ) = refs
    step = pl.program_id(0)
    steps = pl.num_programs(0)
    width = hat_in.shape[0]
    self_part = slice(0, 3 * width)
    out_part = slice(3 * width, 4 * width)
    query_part = slice(4 * width, 5 * width)
    gain_part = slice(5 * width, 6 * width)
    bias_part = slice(6 * width, 7 * width)

    @pl.when(step == 0)
    def _():
        sums[...] = jnp.zeros_like(sums) if first_call else carry[...]
        left = jnp.where(same_head(width), grad_state_in[0, :width], 0.0)
        grad_self_state[0] = flip(left).astype(bf16)
        grad_self_state[1] = left.astype(bf16)
        column = totals_column(grad_state_in[0, width : width + HEADS], width)
        grad_totals[...] = jnp.broadcast_to(column[:, 0:1], grad_totals.shape)

    chunks = [slice(start, start + CHUNK) for start in range(0, hat_in.shape[1], CHUNK)]
    grad_first_of = {}

    def self_back(cols):
        def dots():
            return (
                nn(grad_self_state[0], values_in[:, cols]),
                nn(grad_self_state[1], keys_in[:, cols]),
            )

        def work(grad_keys, grad_values):
            grad_keys = softmax_back(keys_in[:, cols], grad_keys + grad_totals[...])
            three_keep[:width, cols] = grad_q_in[:, cols]
            three_keep[width : 2 * width, cols] = grad_keys.astype(bf16)
            three_keep[2 * width :, cols] = grad_values.astype(bf16)

        return dots, work

    def join(cols):
        def dots():
            return (nn(weights[:, self_part], three_keep[:, cols]),)

        def work(value):
            grad_first = grad_second_in[:, cols].astype(f32) + value
            grad_first_of[cols.start] = grad_first
            cross_keep[:, cols] = grad_first.astype(bf16)

        return dots, work

    def cross_back(cols):
        def dots():
            return nn(weights[:, out_part], cross_keep[:, cols]), nn(state_t[0], queries_in[:, cols])

        def work(share, both):
            undo = inverse(both[funcs * width :])
            sums_by_head = []
            for func in range(funcs):
                span = slice(func * width, (func + 1) * width)
                scales = undo[func * HEADS : (func + 1) * HEADS]
                part = by_head(share, scales)
                stack_keep[span, cols] = part.astype(bf16)
                sums_by_head.append(head_sums(part * by_head(both[span], scales)))
            spare = stack_keep.shape[0] - funcs * (width + HEADS)
            if spare:
                sums_by_head.append(jnp.zeros((spare, CHUNK), f32))
            stack_keep[funcs * width :, cols] = jnp.concatenate(sums_by_head, axis=0).astype(bf16)

        return dots, work

    def query_back(cols):
        def dots():
            return (nn(state[0, :, : stack_keep.shape[0]], stack_keep[:, cols]),)

        def work(grad_q):
            query_keep[:, cols] = softmax_back(queries_in[:, cols], grad_q).astype(bf16)

        return dots, work

    def finish(cols):
        def dots():
            return (nn(weights[:, query_part], query_keep[:, cols]),)

        def work(grad_normed):
            hat, scale = hat_in[:, cols].astype(f32), scale_in[0:1, cols]
            sums[gain_part] += lane_fold(grad_normed * hat)
            sums[bias_part] += lane_fold(grad_normed)
            grad_rows = grad_first_of[cols.start] + norm_back(
                grad_normed * gain_one[...], hat, scale
            )
            grad_tokens[cols, :] = flip(grad_rows)

        return dots, work

    @pl.when(step == 0)
    def _():
        grad_state_sum[...] = jnp.zeros_like(grad_state_sum)

    every = slice(None)
    sum_self = (lambda: (nt(three_keep[...], first_in[...]),), add_to(sums, self_part))
    sum_out = (lambda: (nt(cross_in[...], cross_keep[...]),), add_to(sums, out_part))
    sum_state = (lambda: (nt(stack_keep[...], queries_in[...]),), add_to(grad_state_sum, every))
    sum_query = (lambda: (nt(normed_in[...], query_keep[...]),), add_to(sums, query_part))
    tasks = [stage(cols) for stage in (self_back, join) for cols in chunks]
    tasks += mix([cross_back(cols) for cols in chunks], [sum_self])
    tasks += mix([query_back(cols) for cols in chunks], [sum_out])
    tasks += mix([finish(cols) for cols in chunks], [sum_state])
    run_tasks(tasks + [sum_query])

    @pl.when(step == steps - 1)
    def _():
        mask = same_head(width)
        for func in range(funcs):
            weight = function_weight(presence, item, func, funcs, (1, width))
            left = jnp.where(mask, grad_state_sum[func * width : (func + 1) * width], 0.0)
            grad_cross_state_out[func] = (left * weight).astype(bf16)
            start = funcs * width + func * HEADS
            grad_totals_out[func] = totals_column(grad_state_sum[start : start + HEADS], width)
        sums_out[...] = sums[...]


def points_back(points, keys_in, values_in, grad_state, grad_totals, carry, _after, *refs, shards):
    outs = refs[:shards]
    sums, stage, grads = refs[shards:]
    step = pl.program_id(0)
    width = points.shape[2]
    piece = width // shards

    funcs, slots, _ = points.shape
    chunks = [slice(start, start + CHUNK) for start in range(0, slots, CHUNK)]
    turned = [flip(grad_state[func]) for func in range(funcs)]

    def back(func, cols):
        def dots():
            return (
                nn(turned[func], values_in[func, :, cols]),
                nn(grad_state[func], keys_in[func, :, cols]),
            )

        def work(grad_keys, grad_values):
            grad_keys = grad_keys + grad_totals[func, :, 0:1]
            grad_k = softmax_back(keys_in[func, :, cols], grad_keys)
            grads[func, :width, cols] = grad_k.astype(bf16)
            grads[func, width:, cols] = grad_values.astype(bf16)

        return dots, work

    run_tasks([back(func, cols) for func in range(funcs) for cols in chunks])
    found = nn(grads[0], points[0])
    for func in range(1, funcs):
        found = found + nn(grads[func], points[func])

    @pl.when(step == 0)
    def _():
        sums[...] = found
        gain = as_row(carry[5 * width : 6 * width])
        bias = as_row(carry[6 * width : 7 * width])
        row = lax.broadcasted_iota(jnp.int32, (16, width), 0)
        small = jnp.where(row == 0, gain[:16], bias[:16]).astype(bf16)
        for place in range(5):
            part = carry[place * width : (place + 1) * width]
            part = (flip(part) if place < 3 else part).astype(bf16)
            stage[:, place * piece : (place + 1) * piece, :] = part.reshape(shards, piece, width)
        for shard in range(shards):
            stage[shard, 5 * piece : 5 * piece + 16, :] = small

    @pl.when(step > 0)
    def _():
        sums[...] += found

    @pl.when(step == pl.num_programs(0) - 1)
    def _():
        for place in range(2):
            start = 5 * piece + 16 + place * piece
            part = flip(sums[place * width : (place + 1) * width]).astype(bf16)
            stage[:, start : start + piece, :] = part.reshape(shards, piece, width)
        scatter_blocks(stage, outs)


def total_of(parts):
    value = parts[0][...].astype(f32)
    for part in parts[1:]:
        value = value + part[...].astype(f32)
    return value


def unpack_kernel(*refs, counts, experts, piece, exit_piece, hidden):
    main_parts, parts = refs[: counts[0]], refs[counts[0] : sum(counts)]
    outs, (small, main, rest) = refs[-18:-3], refs[-3:]
    width = main.shape[1]
    main[...] = total_of(main_parts)
    rest[...] = total_of(parts)
    (
        gain_one,
        bias_one,
        query_one,
        key_one,
        value_one,
        out_one,
        query_two,
        key_two,
        value_two,
        out_two,
        gain_two,
        bias_two,
        enter,
        leave,
        gate,
    ) = outs
    start = 0
    for expert in range(experts):
        for half in range(hidden // width):
            block = main[start : start + piece]
            enter[expert, :, half * width : (half + 1) * width] = block
            start += piece
    for expert in range(experts):
        leave[expert] = main[start : start + exit_piece]
        start += exit_piece
    out_two[...] = main[start : start + piece]
    start += piece
    small[:16] = main[start : start + 16]
    start = 0
    for out in (query_two, key_two, value_two, out_one, query_one):
        out[...] = rest[start : start + piece]
        start += piece
    small[16:] = rest[start : start + 16]
    start += 16
    for out in (key_one, value_one):
        out[...] = rest[start : start + piece]
        start += piece
    shard = lax.axis_index("fsdp")
    turned = pltpu.roll(small[...], lax.rem(width - shard * piece, width), 1)
    gain_two[...] = turned[0:1, :piece]
    bias_two[...] = turned[1:2, :piece]
    gain_one[...] = turned[16:17, :piece]
    bias_one[...] = turned[17:18, :piece]
    for row in range(2):
        gate[:, row : row + 1] = small[pl.ds(8 + row * experts + shard, 1), 0:1]


def whole_spec(shape):
    return pl.BlockSpec(shape, lambda *_: (0,) * len(shape))


def route(size, shift, digit, stride):
    def target(i):
        own = i // stride % digit
        return i + ((own + shift) % digit - own) * stride

    return [(i, target(i)) for i in range(size)]


def spread(value, axis, size, digit, stride):
    return [value] + [
        lax.ppermute(value, axis, route(size, shift, digit, stride)) for shift in range(1, digit)
    ]


def exchange(values, axis, size, stride):
    digit = len(values)
    return [values[0]] + [
        lax.ppermute(values[shift], axis, route(size, shift, digit, stride))
        for shift in range(1, digit)
    ]


def digits(size):
    found = []
    stride = 1
    while stride < size:
        rest = size // stride
        digit = 2 if stride == 1 and rest % 2 == 0 else 4 if rest % 4 == 0 else rest
        found.append((digit, stride))
        stride *= digit
    return found or [(1, 1)]


def sum_parts(parts):
    return total_of([part.astype(f32) for part in parts]).astype(bf16)


def shards_fn(
    dp,
    shards,
    tokens,
    points,
    coords,
    presence,
    counts,
    cotangent,
    gain_first,
    bias_first,
    query_first,
    key_first,
    value_first,
    out_first,
    query_second,
    key_second,
    value_second,
    out_second,
    gain_second,
    bias_second,
    expert_in,
    expert_out,
    gate_weight,
):
    count, width = tokens.shape
    items, funcs, slots, _ = points.shape
    length = count // items
    experts, piece, hidden = expert_in.shape
    exit_piece = expert_out.shape[1]
    tile, rest_tile = min(MAIN_TILE, length), min(REST_TILE, length)
    steps, rest_steps = length // tile, length // rest_tile
    inner = experts * hidden
    enter_rows = experts * piece * (hidden // width)
    limit = pltpu.CompilerParams(vmem_limit_bytes=VMEM)

    at = {}
    place = 0
    for name, size in (
        ("query_first", piece),
        ("out_first", piece),
        ("query_second", piece),
        ("key_second", piece),
        ("value_second", piece),
        ("out_second", piece),
        ("expert_in", enter_rows),
        ("expert_out", experts * exit_piece),
        ("small", 16),
    ):
        at[name] = place
        place += size
    late_rows_count = place
    early_pack, late_pack = pl.pallas_call(
        pack_kernel,
        out_shape=[
            jax.ShapeDtypeStruct((2 * piece, width), bf16),
            jax.ShapeDtypeStruct((late_rows_count, width), bf16),
        ],
        name="pack",
    )(
        key_first,
        value_first,
        query_first,
        out_first,
        query_second,
        key_second,
        value_second,
        out_second,
        expert_in,
        expert_out,
        *(
            vector.reshape(1, piece)
            for vector in (gain_first, bias_first, gain_second, bias_second)
        ),
        gate_weight,
    )
    early_parts = spread(early_pack, "fsdp", shards, shards, 1)
    late_parts = spread(late_pack, "fsdp", shards, shards, 1)
    late_specs = [whole_spec((late_rows_count, width))] * shards
    gathered = pltpu.VMEM((shards, late_rows_count, width), bf16)

    smem = pl.BlockSpec(memory_space=pltpu.SMEM)
    units = items * funcs
    state_rows = funcs * width + -(-funcs * HEADS // PAD) * PAD
    flat_points = points.reshape(units, slots, width)
    state_t, state, keys_one, values_one = pl.pallas_call(
        partial(points_forward, funcs=funcs, shards=shards),
        grid=(items,),
        in_specs=[smem, smem, pl.BlockSpec((funcs, slots, width), lambda u: (u, 0, 0))]
        + [whole_spec((2 * piece, width))] * shards,
        out_specs=[
            pl.BlockSpec((1, state_rows, width), lambda u: (u, 0, 0)),
            pl.BlockSpec((1, width, (funcs + 1) * width), lambda u: (u, 0, 0)),
            pl.BlockSpec((funcs, width, slots), lambda u: (u, 0, 0)),
            pl.BlockSpec((funcs, width, slots), lambda u: (u, 0, 0)),
        ],
        out_shape=[
            jax.ShapeDtypeStruct((items, state_rows, width), bf16),
            jax.ShapeDtypeStruct((items, width, (funcs + 1) * width), bf16),
            jax.ShapeDtypeStruct((units, width, slots), bf16),
            jax.ShapeDtypeStruct((units, width, slots), bf16),
        ],
        scratch_shapes=[
            pltpu.VMEM((shards, 2 * piece, width), bf16),
            pltpu.VMEM((2 * width, width), bf16),
        ],
        compiler_params=limit,
        cost_estimate=cost(8),
        name="points_forward",
    )(counts, presence, flat_points, *early_parts)

    kept = jax.ShapeDtypeStruct((width, count), bf16)
    main_rows = enter_rows + experts * exit_piece + piece + 16

    def early(i, p, j):
        return i * steps + jnp.where(p == 0, j, steps - 1)

    def late(i, p, j):
        return i * steps + jnp.where(p == 0, 0, j)

    early_keep = pl.BlockSpec((width, tile), lambda i, p, j: (0, early(i, p, j)))
    late_keep = pl.BlockSpec((width, tile), lambda i, p, j: (0, late(i, p, j)))
    late_rows = pl.BlockSpec((tile, width), lambda i, p, j: (late(i, p, j), 0))
    (
        result,
        queries_one,
        cross,
        first,
        keys_two,
        values_two,
        grad_q_two,
        grad_second,
        grad_state_two,
        rest_weights,
        rest_vectors,
        normed_one,
        hat_one,
        scale_one,
        *main_grads,
    ) = pl.pallas_call(
        partial(main_kernel, funcs=funcs, experts=experts, shards=shards, at=at),
        grid=(items, 2, steps),
        in_specs=[
            pl.BlockSpec((tile, width), lambda i, p, j: (early(i, p, j), 0)),
            late_rows,
            pl.BlockSpec((2, tile), lambda i, p, j: (0, late(i, p, j))),
            pl.BlockSpec((1, state_rows, width), lambda i, p, j: (i, 0, 0)),
        ]
        + late_specs,
        out_specs=[
            late_rows,
            early_keep,
            early_keep,
            early_keep,
            early_keep,
            early_keep,
            late_keep,
            late_keep,
            pl.BlockSpec((1, width + PAD, width), lambda i, p, j: (i, 0, 0)),
            whole_spec((width, 5 * width)),
            whole_spec((width, CHUNK)),
            early_keep,
            early_keep,
            pl.BlockSpec((8, tile), lambda i, p, j: (0, early(i, p, j))),
        ]
        + [whole_spec((main_rows, width))] * shards,
        out_shape=[
            jax.ShapeDtypeStruct((count, width), bf16),
            kept,
            kept,
            kept,
            kept,
            kept,
            kept,
            kept,
            jax.ShapeDtypeStruct((items, width + PAD, width), f32),
            jax.ShapeDtypeStruct((width, 5 * width), bf16),
            jax.ShapeDtypeStruct((width, CHUNK), f32),
            kept,
            kept,
            jax.ShapeDtypeStruct((8, count), f32),
        ]
        + [jax.ShapeDtypeStruct((main_rows, width), bf16)] * shards,
        scratch_shapes=[
            gathered,
            pltpu.VMEM((shards, main_rows, width), bf16),
            pltpu.VMEM((steps, width, tile), f32),
            pltpu.VMEM((steps, width, tile), bf16),
            pltpu.VMEM((width + PAD, width), f32),
            pltpu.VMEM((width + PAD, width), bf16),
            pltpu.VMEM((width, 2 * width), bf16),
            pltpu.VMEM((width + PAD, width), f32),
            pltpu.VMEM((width, width), bf16),
            pltpu.VMEM((width, width), bf16),
            pltpu.VMEM((3 * width, width), bf16),
            pltpu.VMEM((width, width), bf16),
            pltpu.VMEM((width, width), bf16),
            pltpu.VMEM((inner, width), bf16),
            pltpu.VMEM((width, inner), bf16),
            pltpu.VMEM((inner, width), bf16),
            pltpu.VMEM((width, inner), bf16),
            pltpu.VMEM((width, CHUNK), f32),
            pltpu.VMEM((width, CHUNK), f32),
            pltpu.VMEM((width, CHUNK), f32),
            pltpu.VMEM((width, CHUNK), f32),
            pltpu.VMEM((inner, min(2 * GROUP, tile)), bf16),
            pltpu.VMEM((inner, min(2 * GROUP, tile)), bf16),
            pltpu.VMEM((width, tile), bf16),
            pltpu.VMEM((width, tile), bf16),
            pltpu.VMEM((width, tile), bf16),
            pltpu.VMEM((width + PAD, tile), bf16),
            pltpu.VMEM((inner, width), f32),
            pltpu.VMEM((inner, width), f32),
            pltpu.VMEM((width, width), f32),
            pltpu.VMEM((width, width), f32),
            pltpu.VMEM((width, width), f32),
            pltpu.VMEM((2 * experts, tile), f32),
        ],
        compiler_params=limit,
        cost_estimate=cost(80),
        name="main",
    )(tokens, cotangent, coords, state_t, *late_parts)

    rest_rows = 7 * piece + 16

    def rest_call(item, earlier, after):
        first_call = item == 0
        keep_spec = pl.BlockSpec((width, rest_tile), lambda j: (0, item * rest_steps + j))
        row_spec = pl.BlockSpec((rest_tile, width), lambda j: (item * rest_steps + j, 0))
        unit_spec = pl.BlockSpec((funcs, width, width), lambda j: (item, 0, 0))
        anywhere = pl.BlockSpec(memory_space=pl.ANY)
        in_specs = [
            smem,
            keep_spec,
            pl.BlockSpec((8, rest_tile), lambda j: (0, item * rest_steps + j)),
            keep_spec,
            keep_spec,
            keep_spec,
            keep_spec,
            keep_spec,
            keep_spec,
            keep_spec,
            keep_spec,
            pl.BlockSpec((1, width + PAD, width), lambda j: (item, 0, 0)),
            pl.BlockSpec((1, state_rows, width), lambda j: (item, 0, 0)),
            pl.BlockSpec((1, width, (funcs + 1) * width), lambda j: (item, 0, 0)),
            whole_spec((width, 5 * width)),
            whole_spec((width, CHUNK)),
        ]
        operands = [
            presence,
            hat_one,
            scale_one,
            normed_one,
            queries_one,
            cross,
            first,
            keys_two,
            values_two,
            grad_q_two,
            grad_second,
            grad_state_two,
            state_t,
            state,
            rest_weights,
            rest_vectors,
        ]
        aliases = {}
        if not first_call:
            aliases = {len(operands) + k: k for k in range(3)}
            in_specs += [anywhere] * 3 + [whole_spec((7 * width, width)), anywhere]
            operands += [*earlier, after]
        out_specs = [row_spec, unit_spec, unit_spec, whole_spec((7 * width, width))]
        out_shape = [
            jax.ShapeDtypeStruct((count, width), f32),
            jax.ShapeDtypeStruct((units, width, width), bf16),
            jax.ShapeDtypeStruct((units, width, width), f32),
            jax.ShapeDtypeStruct((7 * width, width), f32),
        ]
        return pl.pallas_call(
            partial(
                rest_kernel,
                funcs=funcs,
                item=item,
                first_call=first_call,
            ),
            grid=(rest_steps,),
            in_specs=in_specs,
            out_specs=out_specs,
            out_shape=out_shape,
            input_output_aliases=aliases,
            scratch_shapes=[
                pltpu.VMEM((2, width, width), bf16),
                pltpu.VMEM((width, CHUNK), f32),
                pltpu.VMEM((state_rows, width), f32),
                pltpu.VMEM((7 * width, width), f32),
                pltpu.VMEM((3 * width, rest_tile), bf16),
                pltpu.VMEM((width, rest_tile), bf16),
                pltpu.VMEM((state_rows, rest_tile), bf16),
                pltpu.VMEM((width, rest_tile), bf16),
            ],
            compiler_params=limit,
            cost_estimate=cost(18),
            name="rest",
        )(*operands)

    levels = digits(dp)
    main_levels = levels[::-1]
    main_parts = exchange(main_grads, "fsdp", shards, 1)
    level = 0
    found = None
    for item in range(items):
        found = rest_call(item, found, main_sum if item else None)
        if item < len(main_levels):
            main_sum = sum_parts(main_parts)
            main_parts = spread(main_sum, "dp", dp, *main_levels[item])
            level = item + 1
    grad_tokens, grad_state_one, grad_totals_one, carry = found

    rest_grads = pl.pallas_call(
        partial(points_back, shards=shards),
        grid=(items,),
        in_specs=[
            pl.BlockSpec((funcs, slots, width), lambda u: (u, 0, 0)),
            pl.BlockSpec((funcs, width, slots), lambda u: (u, 0, 0)),
            pl.BlockSpec((funcs, width, slots), lambda u: (u, 0, 0)),
            pl.BlockSpec((funcs, width, width), lambda u: (u, 0, 0)),
            pl.BlockSpec((funcs, width, width), lambda u: (u, 0, 0)),
            whole_spec((7 * width, width)),
            pl.BlockSpec(memory_space=pl.ANY),
        ],
        out_specs=[whole_spec((rest_rows, width))] * shards,
        out_shape=[jax.ShapeDtypeStruct((rest_rows, width), bf16)] * shards,
        scratch_shapes=[
            pltpu.VMEM((2 * width, width), f32),
            pltpu.VMEM((shards, rest_rows, width), bf16),
            pltpu.VMEM((funcs, 2 * width, slots), bf16),
        ],
        compiler_params=limit,
        cost_estimate=cost(7),
        name="points_back",
    )(flat_points, keys_one, values_one, grad_state_one, grad_totals_one, carry, main_sum)
    rest_got = exchange(rest_grads, "fsdp", shards, 1)

    parts = rest_got
    for digit, stride in main_levels[level:]:
        main_parts = spread(sum_parts(main_parts), "dp", dp, digit, stride)
    for digit, stride in levels:
        parts = spread(sum_parts(parts), "dp", dp, digit, stride)

    matrix = jax.ShapeDtypeStruct((piece, width), f32)
    vector = jax.ShapeDtypeStruct((1, piece), f32)
    outs = pl.pallas_call(
        partial(
            unpack_kernel,
            counts=(len(main_parts), len(parts)),
            experts=experts,
            piece=piece,
            exit_piece=exit_piece,
            hidden=hidden,
        ),
        out_shape=[vector] * 2
        + [matrix] * 8
        + [vector] * 2
        + [
            jax.ShapeDtypeStruct(expert_in.shape, f32),
            jax.ShapeDtypeStruct(expert_out.shape, f32),
            jax.ShapeDtypeStruct((1, 2), f32),
        ],
        scratch_shapes=[
            pltpu.VMEM((32, width), f32),
            pltpu.VMEM((main_rows, width), f32),
            pltpu.VMEM((rest_rows, width), f32),
        ],
        name="unpack",
    )(*main_parts, *parts)
    outs = [out.reshape(piece) if out.shape == (1, piece) else out for out in outs]
    return (result, grad_tokens, *outs[:-1], outs[-1].reshape(gate_weight.shape))


def solution(mesh):
    rows = P(("dp", "fsdp"), None)
    matrix = P("fsdp", None)
    vector = P("fsdp")
    expert = P(None, "fsdp", None)
    parameters = (
        (vector, vector)
        + (matrix,) * 8
        + (vector, vector, expert, expert, P(None, "fsdp"))
    )
    return jax.shard_map(
        partial(shards_fn, mesh.shape["dp"], mesh.shape["fsdp"]),
        mesh=mesh,
        in_specs=(
            rows,
            P(("dp", "fsdp"), None, None, None),
            P(None, ("dp", "fsdp")),
            rows,
            rows,
            rows,
        )
        + parameters,
        out_specs=(rows, rows) + parameters,
        check_vma=False,
    )
```

profile of v0, /device:TPU:0, one launch (start us, length us, event | category | flops | bytes accessed | tf_op | source)
XLA Modules:
  0.0 127.5 jit_solution(11610458773706005535)
XLA Ops:
  0.7 1.8 %pack.1 = (bf16[64,128]{1,0:T(8,128)(2,1)}, bf16[720,128]{1,0:T(8,128)(2,1)}) custom-call(bf16[32,128]{1,0:T(8,128)(2,1)} %refs_0_.1, bf16[32,128]{1,0:T(8,128)(2,1)} %refs_1_.1, bf16[32,128]{1,0:T(8,128)(2,1)} %refs_2_.1, bf16[32,128]{1,0:T(8,128)(2,1)} %refs_3_.1, bf16[32,128]{1,0:T(8,128)(2,1)} %refs_4_.1, bf16[32,128]{1,0:T(8,128)(2,1)} %refs_5_.1, ...), custom_call_target="tpu_custom_call" | custom-call | tf_op jit(solution)/shard_map/pack/pallas_call | solution.py:1046
  2.9 2.6 %collective-permute-start.1 = (bf16[64,128]{1,0:T(8,128)(2,1)}, bf16[64,128]{1,0:T(8,128)(2,1)S(1)}, u32[]{:S(2)}, u32[]{:S(2)}) collective-permute-start(bf16[64,128]{1,0:T(8,128)(2,1)} %get-tuple-element.68.refs_0_), channel_id=1, source_target_pairs={{0,2},{1,3},{2,0},{3,1},{4,6},{5,7},{6,4},{7,5},{8,10},{9,11},{10,... | collective-permute-start | bytes 49160 | tf_op jit(solution)/shard_map/ppermute | solution.py:967
  5.4 1.4 %collective-permute-start.2 = (bf16[64,128]{1,0:T(8,128)(2,1)}, bf16[64,128]{1,0:T(8,128)(2,1)S(1)}, u32[]{:S(2)}, u32[]{:S(2)}) collective-permute-start(bf16[64,128]{1,0:T(8,128)(2,1)} %get-tuple-element.68.refs_0_), channel_id=1, source_target_pairs={{0,3},{1,0},{2,1},{3,2},{4,7},{5,4},{6,5},{7,6},{8,11},{9,8},{10,9... | collective-permute-start | bytes 49160 | tf_op jit(solution)/shard_map/ppermute | solution.py:967
  7.3 1.4 %collective-permute-start.5 = (bf16[720,128]{1,0:T(8,128)(2,1)}, bf16[720,128]{1,0:T(8,128)(2,1)S(1)}, u32[]{:S(2)}, u32[]{:S(2)}) collective-permute-start(bf16[720,128]{1,0:T(8,128)(2,1)} %get-tuple-element.70.refs_0_), channel_id=1, source_target_pairs={{0,3},{1,0},{2,1},{3,2},{4,7},{5,4},{6,5},{7,6},{8,11},{9,8},{10,9... | collective-permute-start | bytes 552968 | tf_op jit(solution)/shard_map/ppermute | solution.py:967
  9.3 4.9 %points_forward.1 = (bf16[2,416,128]{2,1,0:T(8,128)(2,1)}, bf16[2,128,512]{2,1,0:T(8,128)(2,1)}, bf16[6,128,1024]{2,1,0:T(8,128)(2,1)}, bf16[6,128,1024]{2,1,0:T(8,128)(2,1)}) custom-call(s32[2,3]{1,0:T(2,128)} %counts.1, s32[2,3]{1,0:T(2,128)} %presence.5, bf16[6,1024,128]{2,1,0:T(8,128)(2,1)} %bitcast.14, bf16[64,128]{1,0:T(8,128)(2,1)} %get-tuple-element.68.refs_0_, ...), custom_call_target="tpu_custom_call" | custom-call | flops 8000000000 | bytes 1000000 | tf_op jit(solution)/shard_map/points_forward/pallas_call | solution.py:1079
  14.6 1.5 %collective-permute-done.5.refs_3_ = bf16[720,128]{1,0:T(8,128)(2,1)S(1)} collective-permute-done((bf16[720,128]{1,0:T(8,128)(2,1)}, bf16[720,128]{1,0:T(8,128)(2,1)S(1)}, u32[]{:S(2)}, u32[]{:S(2)}) %collective-permute-start.5) | collective-permute-done | bytes 184352 | tf_op jit(solution)/shard_map/ppermute | solution.py:967
  16.7 49.5 %main.1 = (bf16[8192,128]{1,0:T(8,128)(2,1)}, bf16[128,8192]{1,0:T(8,128)(2,1)}, bf16[128,8192]{1,0:T(8,128)(2,1)}, bf16[128,8192]{1,0:T(8,128)(2,1)}, bf16[128,...) custom-call(bf16[8192,128]{1,0:T(8,128)(2,1)} %tokens.1, ...), custom_call_target="tpu_custom_call" | custom-call | flops 80000000000 | bytes 1000000 | tf_op jit(solution)/shard_map/main/pallas_call | solution.py:1133
  66.3 1.9 %collective-permute-start.8 = (bf16[560,128]{1,0:T(8,128)(2,1)}, bf16[560,128]{1,0:T(8,128)(2,1)S(1)}, u32[]{:S(2)}, u32[]{:S(2)}) collective-permute-start(bf16[560,128]{1,0:T(8,128)(2,1)} %get-tuple-element.93), channel_id=1, source_target_pairs={{0,3},{1,0},{2,1},{3,2},{4,7},{5,4},{6,5},{7,6},{8,11},{9,8},{10,9... | collective-permute-start | bytes 430088 | tf_op jit(solution)/shard_map/ppermute | solution.py:974
  68.1 1.5 %collective-permute-start.7 = (bf16[560,128]{1,0:T(8,128)(2,1)}, bf16[560,128]{1,0:T(8,128)(2,1)S(1)}, u32[]{:S(2)}, u32[]{:S(2)}) collective-permute-start(bf16[560,128]{1,0:T(8,128)(2,1)} %get-tuple-element.92), channel_id=1, source_target_pairs={{0,2},{1,3},{2,0},{3,1},{4,6},{5,7},{6,4},{7,5},{8,10},{9,11},{10,... | collective-permute-start | bytes 430088 | tf_op jit(solution)/shard_map/ppermute | solution.py:974
  69.7 11.4 %rest.2 = (f32[8192,128]{1,0:T(8,128)}, bf16[6,128,128]{2,1,0:T(8,128)(2,1)}, f32[6,128,128]{2,1,0:T(8,128)}, f32[896,128]{1,0:T(8,128)}) custom-call(s32[2,3]{1,0:T(2,128)} %presence.5, bf16[128,8192]{1,0:T(8,128)(2,1)} %get-tuple-element.72.hat_in, f32[8,8192]{1,0:T(8,128)} %get-tuple-element.73.scale_in, bf16[128,8192]{1,0:T(8,128)(2,1)} %get-tuple-element.74.normed_in, ...), custom_call_target="tpu_custom_call" | custom-call | flops 17999998976 | bytes 1000000 | tf_op jit(solution)/shard_map/rest/pallas_call | solution.py:1273
  81.3 3.7 %collective-permute-start.11 = (bf16[560,128]{1,0:T(8,128)(2,1)S(1)}, bf16[560,128]{1,0:T(8,128)(2,1)S(1)}, u32[]{:S(2)}, u32[]{:S(2)}) collective-permute-start(bf16[560,128]{1,0:T(8,128)(2,1)S(1)} %add_convert_fusion.1.refs_4_), channel_id=1, source_target_pairs={{0,24},{4,28},{8,0},{12,4},{16,8},{20,12},{24,16},{28,20},{1,25},{... | collective-permute-start | bytes 430088 | tf_op jit(solution)/shard_map/ppermute | solution.py:967
  84.9 1.0 collective-permute-start.9
  85.9 11.5 %rest.3 = (f32[8192,128]{1,0:T(8,128)}, bf16[6,128,128]{2,1,0:T(8,128)(2,1)}, f32[6,128,128]{2,1,0:T(8,128)}, f32[896,128]{1,0:T(8,128)}) custom-call(s32[2,3]{1,0:T(2,128)} %presence.5, bf16[128,8192]{1,0:T(8,128)(2,1)} %get-tuple-element.72.hat_in, ...), custom_call_target="tpu_custom_call", output_to_operand_aliasing={{0}: (16, {}), {1}: (17, {}), {2}: (18, {})} | custom-call | flops 17999998976 | bytes 1000000 | tf_op jit(solution)/shard_map/rest/pallas_call | solution.py:1273
  98.1 1.7 %add_convert_fusion._after.refs_0_ = bf16[560,128]{1,0:T(8,128)(2,1)} fusion(bf16[560,128]{1,0:T(8,128)(2,1)S(1)} %collective-permute-done.11, bf16[560,128]{1,0:T(8,128)(2,1)S(1)} %collective-permute-done.10, bf16[560,128]{1,0:T(8,128)(2,1)S(1)} %collective-permute-done.9, bf16[560,128]{1,0:T(8,128)(2,1)} %copy-done.1), kind=kLoop, calls=%fused_computation | loop fusion | flops 573440 | bytes 716800 | tf_op jit(solution)/shard_map/convert_element_type | solution.py:991
  99.8 5.7 %points_back.1 = (bf16[240,128]{1,0:T(8,128)(2,1)}, bf16[240,128]{1,0:T(8,128)(2,1)}, bf16[240,128]{1,0:T(8,128)(2,1)}, bf16[240,128]{1,0:T(8,128)(2,1)}) custom-call(bf16[6,1024,128]{2,1,0:T(8,128)(2,1)} %bitcast.15, bf16[6,128,1024]{2,1,0:T(8,128)(2,1)} %get-tuple-element.95.keys_in, bf16[6,128,1024]{2,1,0:T(8,128)(2,1)} %get-tuple-element.96.values_in, ...), custom_call_target="tpu_custom_call" | custom-call | flops 7000000000 | bytes 1000000 | tf_op jit(solution)/shard_map/points_back/pallas_call | solution.py:1313
  106.9 1.8 %collective-permute-done.15 = bf16[240,128]{1,0:T(8,128)(2,1)S(1)} collective-permute-done((bf16[240,128]{1,0:T(8,128)(2,1)}, bf16[240,128]{1,0:T(8,128)(2,1)S(1)}, u32[]{:S(2)}, u32[]{:S(2)}) %collective-permute-start.15) | collective-permute-done | bytes 61472 | tf_op jit(solution)/shard_map/ppermute | solution.py:974
  108.7 2.4 %collective-permute-done.14 = bf16[240,128]{1,0:T(8,128)(2,1)S(1)} collective-permute-done((bf16[240,128]{1,0:T(8,128)(2,1)}, bf16[240,128]{1,0:T(8,128)(2,1)S(1)}, u32[]{:S(2)}, u32[]{:S(2)}) %collective-permute-start.14) | collective-permute-done | bytes 61472 | tf_op jit(solution)/shard_map/ppermute | solution.py:974
  112.2 1.6 %collective-permute-start.16 = (bf16[240,128]{1,0:T(8,128)(2,1)S(1)}, bf16[240,128]{1,0:T(8,128)(2,1)S(1)}, u32[]{:S(2)}, u32[]{:S(2)}) collective-permute-start(bf16[240,128]{1,0:T(8,128)(2,1)S(1)} %add_convert_fusion.3), channel_id=1, source_target_pairs={{0,4},{4,0},{8,12},{12,8},{16,20},{20,16},{24,28},{28,24},{1,5},{5... | collective-permute-start | bytes 184328 | tf_op jit(solution)/shard_map/ppermute | solution.py:967
  114.3 2.8 %collective-permute-done.16 = bf16[240,128]{1,0:T(8,128)(2,1)S(1)} collective-permute-done((bf16[240,128]{1,0:T(8,128)(2,1)S(1)}, bf16[240,128]{1,0:T(8,128)(2,1)S(1)}, u32[]{:S(2)}, u32[]{:S(2)}) %collective-permute-start.16) | collective-permute-done | bytes 61472 | tf_op jit(solution)/shard_map/ppermute | solution.py:967
  117.1 1.9 %collective-permute-start.17 = (bf16[240,128]{1,0:T(8,128)(2,1)S(1)}, bf16[240,128]{1,0:T(8,128)(2,1)S(1)}, u32[]{:S(2)}, u32[]{:S(2)}) collective-permute-start(bf16[240,128]{1,0:T(8,128)(2,1)S(1)} %add_convert_fusion.2.refs_2_), channel_id=1, source_target_pairs={{0,8},{4,12},{8,16},{12,20},{16,24},{20,28},{24,0},{28,4},{1,9},{5... | collective-permute-start | bytes 184328 | tf_op jit(solution)/shard_map/ppermute | solution.py:967
  119.1 1.2 collective-permute-start.18
  120.2 2.5 %collective-permute-start.19 = (bf16[240,128]{1,0:T(8,128)(2,1)S(1)}, bf16[240,128]{1,0:T(8,128)(2,1)S(1)}, u32[]{:S(2)}, u32[]{:S(2)}) collective-permute-start(bf16[240,128]{1,0:T(8,128)(2,1)S(1)} %add_convert_fusion.2.refs_2_), channel_id=1, source_target_pairs={{0,24},{4,28},{8,0},{12,4},{16,8},{20,12},{24,16},{28,20},{1,25},{... | collective-permute-start | bytes 184328 | tf_op jit(solution)/shard_map/ppermute | solution.py:967
  123.2 1.0 collective-permute-done.18.refs_4_
  125.5 1.8 %unpack.1 = (f32[1,32]{1,0:T(1,128)}, f32[1,32]{1,0:T(1,128)}, f32[32,128]{1,0:T(8,128)}, f32[32,128]{1,0:T(8,128)}, f32[32,128]{1,0:T(8,128)}, /*index=5*/f32[3...) custom-call(bf16[560,128]{1,0:T(8,128)(2,1)} %add_convert_fusion._af, ...), custom_call_target="tpu_custom_call" | custom-call | tf_op jit(solution)/shard_map/unpack/pallas_call | solution.py:1346
  (55 shorter events, 7.8 us)
Async XLA Ops:
  2.4 4.8 %collective-permute-start = (bf16[64,128]{1,0:T(8,128)(2,1)}, bf16[64,128]{1,0:T(8,128)(2,1)S(1)}, u32[]{:S(2)}, u32[]{:S(2)}) collective-permute-start(bf16[64,128]{1,0:T(8,128)(2,1)} %get-tuple-element.68.refs_0_), channel_id=1, source_target_pairs={{0,1},{1,2},{2,3},{3,0},{4,5},{5,6},{6,7},{7,4},{8,9},{9,10},{10,1... | collective-permute-start | bytes 49160 | tf_op jit(solution)/shard_map/ppermute | solution.py:967
  2.9 5.8 %collective-permute-start.1 = (bf16[64,128]{1,0:T(8,128)(2,1)}, bf16[64,128]{1,0:T(8,128)(2,1)S(1)}, u32[]{:S(2)}, u32[]{:S(2)}) collective-permute-start(bf16[64,128]{1,0:T(8,128)(2,1)} %get-tuple-element.68.refs_0_), channel_id=1, source_target_pairs={{0,2},{1,3},{2,0},{3,1},{4,6},{5,7},{6,4},{7,5},{8,10},{9,11},{10,... | collective-permute-start | bytes 49160 | tf_op jit(solution)/shard_map/ppermute | solution.py:967
  5.4 3.2 %collective-permute-start.2 = (bf16[64,128]{1,0:T(8,128)(2,1)}, bf16[64,128]{1,0:T(8,128)(2,1)S(1)}, u32[]{:S(2)}, u32[]{:S(2)}) collective-permute-start(bf16[64,128]{1,0:T(8,128)(2,1)} %get-tuple-element.68.refs_0_), channel_id=1, source_target_pairs={{0,3},{1,0},{2,1},{3,2},{4,7},{5,4},{6,5},{7,6},{8,11},{9,8},{10,9... | collective-permute-start | bytes 49160 | tf_op jit(solution)/shard_map/ppermute | solution.py:967
  6.9 7.3 %collective-permute-start.3 = (bf16[720,128]{1,0:T(8,128)(2,1)}, bf16[720,128]{1,0:T(8,128)(2,1)S(1)}, u32[]{:S(2)}, u32[]{:S(2)}) collective-permute-start(bf16[720,128]{1,0:T(8,128)(2,1)} %get-tuple-element.70.refs_0_), channel_id=1, source_target_pairs={{0,1},{1,2},{2,3},{3,0},{4,5},{5,6},{6,7},{7,4},{8,9},{9,10},{10,1... | collective-permute-start | bytes 552968 | tf_op jit(solution)/shard_map/ppermute | solution.py:967
  6.9 7.7 %collective-permute-start.4 = (bf16[720,128]{1,0:T(8,128)(2,1)}, bf16[720,128]{1,0:T(8,128)(2,1)S(1)}, u32[]{:S(2)}, u32[]{:S(2)}) collective-permute-start(bf16[720,128]{1,0:T(8,128)(2,1)} %get-tuple-element.70.refs_0_), channel_id=1, source_target_pairs={{0,2},{1,3},{2,0},{3,1},{4,6},{5,7},{6,4},{7,5},{8,10},{9,11},{10,... | collective-permute-start | bytes 552968 | tf_op jit(solution)/shard_map/ppermute | solution.py:967
  7.3 8.8 %collective-permute-start.5 = (bf16[720,128]{1,0:T(8,128)(2,1)}, bf16[720,128]{1,0:T(8,128)(2,1)S(1)}, u32[]{:S(2)}, u32[]{:S(2)}) collective-permute-start(bf16[720,128]{1,0:T(8,128)(2,1)} %get-tuple-element.70.refs_0_), channel_id=1, source_target_pairs={{0,3},{1,0},{2,1},{3,2},{4,7},{5,4},{6,5},{7,6},{8,11},{9,8},{10,9... | collective-permute-start | bytes 552968 | tf_op jit(solution)/shard_map/ppermute | solution.py:967
  66.3 14.9 %collective-permute-start.8 = (bf16[560,128]{1,0:T(8,128)(2,1)}, bf16[560,128]{1,0:T(8,128)(2,1)S(1)}, u32[]{:S(2)}, u32[]{:S(2)}) collective-permute-start(bf16[560,128]{1,0:T(8,128)(2,1)} %get-tuple-element.93), channel_id=1, source_target_pairs={{0,3},{1,0},{2,1},{3,2},{4,7},{5,4},{6,5},{7,6},{8,11},{9,8},{10,9... | collective-permute-start | bytes 430088 | tf_op jit(solution)/shard_map/ppermute | solution.py:974
  68.1 13.0 %collective-permute-start.7 = (bf16[560,128]{1,0:T(8,128)(2,1)}, bf16[560,128]{1,0:T(8,128)(2,1)S(1)}, u32[]{:S(2)}, u32[]{:S(2)}) collective-permute-start(bf16[560,128]{1,0:T(8,128)(2,1)} %get-tuple-element.92), channel_id=1, source_target_pairs={{0,2},{1,3},{2,0},{3,1},{4,6},{5,7},{6,4},{7,5},{8,10},{9,11},{10,... | collective-permute-start | bytes 430088 | tf_op jit(solution)/shard_map/ppermute | solution.py:974
  69.7 11.5 %collective-permute-start.6 = (bf16[560,128]{1,0:T(8,128)(2,1)}, bf16[560,128]{1,0:T(8,128)(2,1)S(1)}, u32[]{:S(2)}, u32[]{:S(2)}) collective-permute-start(bf16[560,128]{1,0:T(8,128)(2,1)} %get-tuple-element.91), channel_id=1, source_target_pairs={{0,1},{1,2},{2,3},{3,0},{4,5},{5,6},{6,7},{7,4},{8,9},{9,10},{10,1... | collective-permute-start | bytes 430088 | tf_op jit(solution)/shard_map/ppermute | solution.py:974
  69.7 11.5 %copy-start.4 = (bf16[560,128]{1,0:T(8,128)(2,1)S(1)}, bf16[560,128]{1,0:T(8,128)(2,1)}, u32[]{:S(2)}) copy-start(bf16[560,128]{1,0:T(8,128)(2,1)} %get-tuple-element.90) | copy-start | bytes 430084
  81.2 4.7 %copy-start.1 = (bf16[560,128]{1,0:T(8,128)(2,1)}, bf16[560,128]{1,0:T(8,128)(2,1)S(1)}, u32[]{:S(2)}) copy-start(bf16[560,128]{1,0:T(8,128)(2,1)S(1)} %add_convert_fusion.1.refs_4_) | copy-start | bytes 430084
  81.3 16.2 %collective-permute-start.11 = (bf16[560,128]{1,0:T(8,128)(2,1)S(1)}, bf16[560,128]{1,0:T(8,128)(2,1)S(1)}, u32[]{:S(2)}, u32[]{:S(2)}) collective-permute-start(bf16[560,128]{1,0:T(8,128)(2,1)S(1)} %add_convert_fusion.1.refs_4_), channel_id=1, source_target_pairs={{0,24},{4,28},{8,0},{12,4},{16,8},{20,12},{24,16},{28,20},{1,25},{... | collective-permute-start | bytes 430088 | tf_op jit(solution)/shard_map/ppermute | solution.py:967
  84.9 13.2 %collective-permute-start.10 = (bf16[560,128]{1,0:T(8,128)(2,1)S(1)}, bf16[560,128]{1,0:T(8,128)(2,1)S(1)}, u32[]{:S(2)}, u32[]{:S(2)}) collective-permute-start(bf16[560,128]{1,0:T(8,128)(2,1)S(1)} %add_convert_fusion.1.refs_4_), channel_id=1, source_target_pairs={{0,16},{4,20},{8,24},{12,28},{16,0},{20,4},{24,8},{28,12},{1,17},{... | collective-permute-start | bytes 430088 | tf_op jit(solution)/shard_map/ppermute | solution.py:967
  84.9 13.2 %collective-permute-start.9 = (bf16[560,128]{1,0:T(8,128)(2,1)S(1)}, bf16[560,128]{1,0:T(8,128)(2,1)S(1)}, u32[]{:S(2)}, u32[]{:S(2)}) collective-permute-start(bf16[560,128]{1,0:T(8,128)(2,1)S(1)} %add_convert_fusion.1.refs_4_), channel_id=1, source_target_pairs={{0,8},{4,12},{8,16},{12,20},{16,24},{20,28},{24,0},{28,4},{1,9},{5... | collective-permute-start | bytes 430088 | tf_op jit(solution)/shard_map/ppermute | solution.py:967
  99.8 14.0 %copy-start = (bf16[560,128]{1,0:T(8,128)(2,1)S(1)}, bf16[560,128]{1,0:T(8,128)(2,1)}, u32[]{:S(2)}) copy-start(bf16[560,128]{1,0:T(8,128)(2,1)} %add_convert_fusion._after.refs_0_) | copy-start | bytes 430084
  105.5 3.2 %collective-permute-start.15 = (bf16[240,128]{1,0:T(8,128)(2,1)}, bf16[240,128]{1,0:T(8,128)(2,1)S(1)}, u32[]{:S(2)}, u32[]{:S(2)}) collective-permute-start(bf16[240,128]{1,0:T(8,128)(2,1)} %get-tuple-element.103), channel_id=1, source_target_pairs={{0,3},{1,0},{2,1},{3,2},{4,7},{5,4},{6,5},{7,6},{8,11},{9,8},{10,9... | collective-permute-start | bytes 184328 | tf_op jit(solution)/shard_map/ppermute | solution.py:974
  106.2 5.0 %collective-permute-start.14 = (bf16[240,128]{1,0:T(8,128)(2,1)}, bf16[240,128]{1,0:T(8,128)(2,1)S(1)}, u32[]{:S(2)}, u32[]{:S(2)}) collective-permute-start(bf16[240,128]{1,0:T(8,128)(2,1)} %get-tuple-element.102), channel_id=1, source_target_pairs={{0,2},{1,3},{2,0},{3,1},{4,6},{5,7},{6,4},{7,5},{8,10},{9,11},{10,... | collective-permute-start | bytes 184328 | tf_op jit(solution)/shard_map/ppermute | solution.py:974
  106.9 4.4 %collective-permute-start.13 = (bf16[240,128]{1,0:T(8,128)(2,1)}, bf16[240,128]{1,0:T(8,128)(2,1)S(1)}, u32[]{:S(2)}, u32[]{:S(2)}) collective-permute-start(bf16[240,128]{1,0:T(8,128)(2,1)} %get-tuple-element.101), channel_id=1, source_target_pairs={{0,1},{1,2},{2,3},{3,0},{4,5},{5,6},{6,7},{7,4},{8,9},{9,10},{10,1... | collective-permute-start | bytes 184328 | tf_op jit(solution)/shard_map/ppermute | solution.py:974
  112.2 4.9 %collective-permute-start.16 = (bf16[240,128]{1,0:T(8,128)(2,1)S(1)}, bf16[240,128]{1,0:T(8,128)(2,1)S(1)}, u32[]{:S(2)}, u32[]{:S(2)}) collective-permute-start(bf16[240,128]{1,0:T(8,128)(2,1)S(1)} %add_convert_fusion.3), channel_id=1, source_target_pairs={{0,4},{4,0},{8,12},{12,8},{16,20},{20,16},{24,28},{28,24},{1,5},{5... | collective-permute-start | bytes 184328 | tf_op jit(solution)/shard_map/ppermute | solution.py:967
  113.8 9.0 %collective-permute-start.12 = (bf16[560,128]{1,0:T(8,128)(2,1)S(1)}, bf16[560,128]{1,0:T(8,128)(2,1)S(1)}, u32[]{:S(2)}, u32[]{:S(2)}) collective-permute-start(bf16[560,128]{1,0:T(8,128)(2,1)S(1)} %copy-done), channel_id=1, source_target_pairs={{0,4},{4,0},{8,12},{12,8},{16,20},{20,16},{24,28},{28,24},{1,5},{5... | collective-permute-start | bytes 430088 | tf_op jit(solution)/shard_map/ppermute | solution.py:967
  117.1 7.7 %copy-start.2 = (bf16[240,128]{1,0:T(8,128)(2,1)}, bf16[240,128]{1,0:T(8,128)(2,1)S(1)}, u32[]{:S(2)}) copy-start(bf16[240,128]{1,0:T(8,128)(2,1)S(1)} %add_convert_fusion.2.refs_2_) | copy-start | bytes 184324
  117.1 6.1 %collective-permute-start.17 = (bf16[240,128]{1,0:T(8,128)(2,1)S(1)}, bf16[240,128]{1,0:T(8,128)(2,1)S(1)}, u32[]{:S(2)}, u32[]{:S(2)}) collective-permute-start(bf16[240,128]{1,0:T(8,128)(2,1)S(1)} %add_convert_fusion.2.refs_2_), channel_id=1, source_target_pairs={{0,8},{4,12},{8,16},{12,20},{16,24},{20,28},{24,0},{28,4},{1,9},{5... | collective-permute-start | bytes 184328 | tf_op jit(solution)/shard_map/ppermute | solution.py:967
  119.1 5.2 %collective-permute-start.18 = (bf16[240,128]{1,0:T(8,128)(2,1)S(1)}, bf16[240,128]{1,0:T(8,128)(2,1)S(1)}, u32[]{:S(2)}, u32[]{:S(2)}) collective-permute-start(bf16[240,128]{1,0:T(8,128)(2,1)S(1)} %add_convert_fusion.2.refs_2_), channel_id=1, source_target_pairs={{0,16},{4,20},{8,24},{12,28},{16,0},{20,4},{24,8},{28,12},{1,17},{... | collective-permute-start | bytes 184328 | tf_op jit(solution)/shard_map/ppermute | solution.py:967
  120.2 4.6 %collective-permute-start.19 = (bf16[240,128]{1,0:T(8,128)(2,1)S(1)}, bf16[240,128]{1,0:T(8,128)(2,1)S(1)}, u32[]{:S(2)}, u32[]{:S(2)}) collective-permute-start(bf16[240,128]{1,0:T(8,128)(2,1)S(1)} %add_convert_fusion.2.refs_2_), channel_id=1, source_target_pairs={{0,24},{4,28},{8,0},{12,4},{16,8},{20,12},{24,16},{28,20},{1,25},{... | collective-permute-start | bytes 184328 | tf_op jit(solution)/shard_map/ppermute | solution.py:967
  (10 other events, 11.7 us)
where the time goes:
time: 128 us; the launch traced here: 127 us
  Pallas kernels  86.7 us (68%)
  starting transfers between devices  23.4 us (18%)
  waiting for transfers between devices  11.8 us (9%)
  other arithmetic  2.62 us (2%)
  local copies, waits for them, and re-layouts  1.9 us (1%)
    pallas_call x1, Pallas kernels, shards_fn(): pl.pallas_call(partial(main_kernel, funcs=funcs, experts=experts, shards=...  49.5 us
    pallas_call x2, Pallas kernels, rest_call(): pl.pallas_call(partial(rest_kernel, funcs=funcs, item=item, first_call=fi...  23 us
    ppermute x14, starting transfers between devices, spread(): lax.ppermute(value, axis, route(size, shift, digit, stride))  18.6 us
    ppermute x14, waiting for transfers between devices, spread(): lax.ppermute(value, axis, route(size, shift, digit, stride))  7.44 us
    pallas_call x1, Pallas kernels, shards_fn(): pl.pallas_call(partial(points_back, shards=shards), grid=(items,), in_spe...  5.73 us
    pallas_call x1, Pallas kernels, shards_fn(): pl.pallas_call(partial(points_forward, funcs=funcs, shards=shards), grid=...  4.89 us
    ppermute x6, starting transfers between devices, exchange(): lax.ppermute(values[shift], axis, route(size, shift, digit, stride))  4.79 us
    ppermute x6, waiting for transfers between devices, exchange(): lax.ppermute(values[shift], axis, route(size, shift, digit, stride))  4.39 us
  transfers between devices with their start and end apart: 20, of which 10 were waited for; matrix products, arithmetic and copies ran while one was open for 0% of the time, Pallas kernels for 22%

commit v1 on v0

--- a/solution.py
+++ b/solution.py
@@ -15,7 +15,7 @@
 MAIN_TILE = 4096
 REST_TILE = 1024
 GROUP = 1024
-STRIP = 128
+STRIP = 256
 CHUNK = 256
 SLAB = 64
 PAD = 16
@@ -1097,7 +1097,7 @@
             pltpu.VMEM((shards, 2 * piece, width), bf16),
             pltpu.VMEM((2 * width, width), bf16),
         ],
-        compiler_params=limit,
+        compiler_params=pltpu.CompilerParams(vmem_limit_bytes=VMEM * 2 // 5),
         cost_estimate=cost(8),
         name="points_forward",
     )(counts, presence, flat_points, *early_parts)
@@ -1365,6 +1365,7 @@
             pltpu.VMEM((main_rows, width), f32),
             pltpu.VMEM((rest_rows, width), f32),
         ],
+        compiler_params=pltpu.CompilerParams(vmem_limit_bytes=VMEM // 8),
         name="unpack",
     )(*main_parts, *parts)
     outs = [out.reshape(piece) if out.shape == (1, piece) else out for out in outs]

time: 128 us -> 129 us (level)
  local copies, waits for them, and re-layouts: 1.9 us -> 7.96 us
  Pallas kernels: 86.7 us -> 84.5 us
  waiting for transfers between devices: 11.8 us -> 9.89 us
    unnamed x28, local copies, waits for them, and re-layouts: 1.9 us -> 7.96 us
    pallas_call x1, Pallas kernels: 4.89 us -> 3.26 us  [shards_fn(): pl.pallas_call(partial(points_forward, funcs=funcs, shards=shards), grid=...]
    ppermute x14, waiting for transfers between devices: 7.44 us -> 6 us  [spread(): lax.ppermute(value, axis, route(size, shift, digit, stride))]
  transfers between devices with their start and end apart: 20 -> 20, of which waited for: 10 -> 7; matrix products, arithmetic and copies ran while one was open for 0% -> 0% of each run, Pallas kernels for 22% -> 20%
where the time goes in v1:
time: 129 us
  Pallas kernels  84.5 us (66%)
  starting transfers between devices  23 us (18%)
  waiting for transfers between devices  9.89 us (8%)
  local copies, waits for them, and re-layouts  7.96 us (6%)
  other arithmetic  2.62 us (2%)
    pallas_call x1, Pallas kernels, shards_fn(): pl.pallas_call(partial(main_kernel, funcs=funcs, experts=experts, shards=...  50.1 us
    pallas_call x2, Pallas kernels, rest_call(): pl.pallas_call(partial(rest_kernel, funcs=funcs, item=item, first_call=fi...  23 us
    ppermute x14, starting transfers between devices, spread(): lax.ppermute(value, axis, route(size, shift, digit, stride))  18.5 us
    unnamed x28, local copies, waits for them, and re-layouts  7.96 us
    ppermute x14, waiting for transfers between devices, spread(): lax.ppermute(value, axis, route(size, shift, digit, stride))  6 us
    pallas_call x1, Pallas kernels, shards_fn(): pl.pallas_call(partial(points_back, shards=shards), grid=(items,), in_spe...  5.72 us
    ppermute x6, starting transfers between devices, exchange(): lax.ppermute(values[shift], axis, route(size, shift, digit, stride))  4.45 us
    ppermute x6, waiting for transfers between devices, exchange(): lax.ppermute(values[shift], axis, route(size, shift, digit, stride))  3.89 us
  transfers between devices with their start and end apart: 20, of which 7 were waited for; matrix products, arithmetic and copies ran while one was open for 0% of the time, Pallas kernels for 20%

profile of v1, /device:TPU:0, one launch (start us, length us, event | category | flops | bytes accessed | tf_op | source)
XLA Modules:
  0.0 129.0 jit_solution(8485788961122624639)
XLA Ops:
  0.7 1.8 %pack.1 = (bf16[64,128]{1,0:T(8,128)(2,1)}, bf16[720,128]{1,0:T(8,128)(2,1)}) custom-call(bf16[32,128]{1,0:T(8,128)(2,1)} %refs_0_.1, bf16[32,128]{1,0:T(8,128)(2,1)} %refs_1_.1, bf16[32,128]{1,0:T(8,128)(2,1)} %refs_2_.1, bf16[32,128]{1,0:T(8,128)(2,1)} %refs_3_.1, bf16[32,128]{1,0:T(8,128)(2,1)} %refs_4_.1, bf16[32,128]{1,0:T(8,128)(2,1)} %refs_5_.1, ...), custom_call_target="tpu_custom_call" | custom-call | tf_op jit(solution)/shard_map/pack/pallas_call | solution.py:1046
  2.9 2.6 %collective-permute-start.1 = (bf16[64,128]{1,0:T(8,128)(2,1)}, bf16[64,128]{1,0:T(8,128)(2,1)S(1)}, u32[]{:S(2)}, u32[]{:S(2)}) collective-permute-start(bf16[64,128]{1,0:T(8,128)(2,1)} %get-tuple-element.68.refs_0_), channel_id=1, source_target_pairs={{0,2},{1,3},{2,0},{3,1},{4,6},{5,7},{6,4},{7,5},{8,10},{9,11},{10,... | collective-permute-start | bytes 49160 | tf_op jit(solution)/shard_map/ppermute | solution.py:967
  5.4 1.4 %collective-permute-start.2 = (bf16[64,128]{1,0:T(8,128)(2,1)}, bf16[64,128]{1,0:T(8,128)(2,1)S(1)}, u32[]{:S(2)}, u32[]{:S(2)}) collective-permute-start(bf16[64,128]{1,0:T(8,128)(2,1)} %get-tuple-element.68.refs_0_), channel_id=1, source_target_pairs={{0,3},{1,0},{2,1},{3,2},{4,7},{5,4},{6,5},{7,6},{8,11},{9,8},{10,9... | collective-permute-start | bytes 49160 | tf_op jit(solution)/shard_map/ppermute | solution.py:967
  7.3 1.4 %collective-permute-start.5 = (bf16[720,128]{1,0:T(8,128)(2,1)}, bf16[720,128]{1,0:T(8,128)(2,1)S(1)}, u32[]{:S(2)}, u32[]{:S(2)}) collective-permute-start(bf16[720,128]{1,0:T(8,128)(2,1)} %get-tuple-element.70.refs_0_), channel_id=1, source_target_pairs={{0,3},{1,0},{2,1},{3,2},{4,7},{5,4},{6,5},{7,6},{8,11},{9,8},{10,9... | collective-permute-start | bytes 552968 | tf_op jit(solution)/shard_map/ppermute | solution.py:967
  8.7 1.4 %copy-done.1 = bf16[2,3,1024,128]{3,2,1,0:T(8,128)(2,1)S(1)} copy-done((bf16[2,3,1024,128]{3,2,1,0:T(8,128)(2,1)S(1)}, bf16[2,3,1024,128]{3,2,1,0:T(8,128)(2,1)}, u32[]{:S(2)}) %copy-start.1) | copy-done | bytes 1572888
  12.1 3.3 %points_forward.1 = (bf16[2,416,128]{2,1,0:T(8,128)(2,1)S(1)}, bf16[2,128,512]{2,1,0:T(8,128)(2,1)S(1)}, bf16[6,128,1024]{2,1,0:T(8,128)(2,1)S(1)}, bf16[6,128,1024]{2,1,0:T(8,128)(2,1)S(1)}) custom-call(s32[2,3]{1,0:T(2,128)S(1)} %copy-done.3, s32[2,3]{1,0:T(2,128)S(1)} %copy-done.4, bf16[6,1024,128]{2,1,0:T(8,128)(2,1)S(1)} %bitcast.11, ...), custom_call_target="tpu_custom_call" | custom-call | flops 8000000000 | bytes 1000000 | tf_op jit(solution)/shard_map/points_forward/pallas_call | solution.py:1079
  15.4 1.2 copy-done.5
  16.6 1.1 copy-done.6
  19.9 50.1 %main.1 = (bf16[8192,128]{1,0:T(8,128)(2,1)}, bf16[128,8192]{1,0:T(8,128)(2,1)}, bf16[128,8192]{1,0:T(8,128)(2,1)}, bf16[128,8192]{1,0:T(8,128)(2,1)}, bf16[128,...) custom-call(bf16[8192,128]{1,0:T(8,128)(2,1)} %tokens.1, ...), custom_call_target="tpu_custom_call" | custom-call | flops 80000000000 | bytes 1000000 | tf_op jit(solution)/shard_map/main/pallas_call | solution.py:1133
  70.0 2.1 %collective-permute-start.8 = (bf16[560,128]{1,0:T(8,128)(2,1)}, bf16[560,128]{1,0:T(8,128)(2,1)S(1)}, u32[]{:S(2)}, u32[]{:S(2)}) collective-permute-start(bf16[560,128]{1,0:T(8,128)(2,1)} %get-tuple-element.93), channel_id=1, source_target_pairs={{0,3},{1,0},{2,1},{3,2},{4,7},{5,4},{6,5},{7,6},{8,11},{9,8},{10,9... | collective-permute-start | bytes 430088 | tf_op jit(solution)/shard_map/ppermute | solution.py:974
  72.3 11.4 %rest.2 = (f32[8192,128]{1,0:T(8,128)}, bf16[6,128,128]{2,1,0:T(8,128)(2,1)}, f32[6,128,128]{2,1,0:T(8,128)}, f32[896,128]{1,0:T(8,128)}) custom-call(s32[2,3]{1,0:T(2,128)} %presence.5, bf16[128,8192]{1,0:T(8,128)(2,1)} %get-tuple-element.72.hat_in, f32[8,8192]{1,0:T(8,128)} %get-tuple-element.73.scale_in, bf16[128,8192]{1,0:T(8,128)(2,1)} %get-tuple-element.74.normed_in, ...), custom_call_target="tpu_custom_call" | custom-call | flops 17999998976 | bytes 1000000 | tf_op jit(solution)/shard_map/rest/pallas_call | solution.py:1273
  83.9 3.7 %collective-permute-start.11 = (bf16[560,128]{1,0:T(8,128)(2,1)S(1)}, bf16[560,128]{1,0:T(8,128)(2,1)S(1)}, u32[]{:S(2)}, u32[]{:S(2)}) collective-permute-start(bf16[560,128]{1,0:T(8,128)(2,1)S(1)} %add_convert_fusion.1.refs_4_), channel_id=1, source_target_pairs={{0,24},{4,28},{8,0},{12,4},{16,8},{20,12},{24,16},{28,20},{1,25},{... | collective-permute-start | bytes 430088 | tf_op jit(solution)/shard_map/ppermute | solution.py:967
  87.5 1.0 collective-permute-start.9
  88.6 11.5 %rest.3 = (f32[8192,128]{1,0:T(8,128)}, bf16[6,128,128]{2,1,0:T(8,128)(2,1)}, f32[6,128,128]{2,1,0:T(8,128)}, f32[896,128]{1,0:T(8,128)}) custom-call(s32[2,3]{1,0:T(2,128)} %presence.5, bf16[128,8192]{1,0:T(8,128)(2,1)} %get-tuple-element.72.hat_in, ...), custom_call_target="tpu_custom_call", output_to_operand_aliasing={{0}: (16, {}), {1}: (17, {}), {2}: (18, {})} | custom-call | flops 17999998976 | bytes 1000000 | tf_op jit(solution)/shard_map/rest/pallas_call | solution.py:1273
  100.7 1.7 %add_convert_fusion._after.refs_0_ = bf16[560,128]{1,0:T(8,128)(2,1)} fusion(bf16[560,128]{1,0:T(8,128)(2,1)S(1)} %collective-permute-done.11, bf16[560,128]{1,0:T(8,128)(2,1)S(1)} %collective-permute-done.10, bf16[560,128]{1,0:T(8,128)(2,1)S(1)} %collective-permute-done.9, bf16[560,128]{1,0:T(8,128)(2,1)} %copy-done.9), kind=kLoop, calls=%fused_computation | loop fusion | flops 573440 | bytes 716800 | tf_op jit(solution)/shard_map/convert_element_type | solution.py:991
  102.4 5.7 %points_back.1 = (bf16[240,128]{1,0:T(8,128)(2,1)}, bf16[240,128]{1,0:T(8,128)(2,1)}, bf16[240,128]{1,0:T(8,128)(2,1)}, bf16[240,128]{1,0:T(8,128)(2,1)}) custom-call(bf16[6,1024,128]{2,1,0:T(8,128)(2,1)} %bitcast.10, bf16[6,128,1024]{2,1,0:T(8,128)(2,1)} %copy-done.5, bf16[6,128,1024]{2,1,0:T(8,128)(2,1)} %copy-done.6, ...), custom_call_target="tpu_custom_call" | custom-call | flops 7000000000 | bytes 1000000 | tf_op jit(solution)/shard_map/points_back/pallas_call | solution.py:1313
  108.5 1.8 %collective-permute-start.14 = (bf16[240,128]{1,0:T(8,128)(2,1)}, bf16[240,128]{1,0:T(8,128)(2,1)S(1)}, u32[]{:S(2)}, u32[]{:S(2)}) collective-permute-start(bf16[240,128]{1,0:T(8,128)(2,1)} %get-tuple-element.102), channel_id=1, source_target_pairs={{0,2},{1,3},{2,0},{3,1},{4,6},{5,7},{6,4},{7,5},{8,10},{9,11},{10,... | collective-permute-start | bytes 184328 | tf_op jit(solution)/shard_map/ppermute | solution.py:974
  110.8 2.7 %collective-permute-done.14 = bf16[240,128]{1,0:T(8,128)(2,1)S(1)} collective-permute-done((bf16[240,128]{1,0:T(8,128)(2,1)}, bf16[240,128]{1,0:T(8,128)(2,1)S(1)}, u32[]{:S(2)}, u32[]{:S(2)}) %collective-permute-start.14) | collective-permute-done | bytes 61472 | tf_op jit(solution)/shard_map/ppermute | solution.py:974
  115.0 1.6 %collective-permute-start.16 = (bf16[240,128]{1,0:T(8,128)(2,1)S(1)}, bf16[240,128]{1,0:T(8,128)(2,1)S(1)}, u32[]{:S(2)}, u32[]{:S(2)}) collective-permute-start(bf16[240,128]{1,0:T(8,128)(2,1)S(1)} %add_convert_fusion.3), channel_id=1, source_target_pairs={{0,4},{4,0},{8,12},{12,8},{16,20},{20,16},{24,28},{28,24},{1,5},{5... | collective-permute-start | bytes 184328 | tf_op jit(solution)/shard_map/ppermute | solution.py:967
  117.1 2.5 %collective-permute-done.16 = bf16[240,128]{1,0:T(8,128)(2,1)S(1)} collective-permute-done((bf16[240,128]{1,0:T(8,128)(2,1)S(1)}, bf16[240,128]{1,0:T(8,128)(2,1)S(1)}, u32[]{:S(2)}, u32[]{:S(2)}) %collective-permute-start.16) | collective-permute-done | bytes 61472 | tf_op jit(solution)/shard_map/ppermute | solution.py:967
  119.6 2.5 %collective-permute-start.17 = (bf16[240,128]{1,0:T(8,128)(2,1)S(1)}, bf16[240,128]{1,0:T(8,128)(2,1)S(1)}, u32[]{:S(2)}, u32[]{:S(2)}) collective-permute-start(bf16[240,128]{1,0:T(8,128)(2,1)S(1)} %add_convert_fusion.2.refs_2_), channel_id=1, source_target_pairs={{0,8},{4,12},{8,16},{12,20},{16,24},{20,28},{24,0},{28,4},{1,9},{5... | collective-permute-start | bytes 184328 | tf_op jit(solution)/shard_map/ppermute | solution.py:967
  122.2 1.2 collective-permute-start.18
  123.3 1.8 %collective-permute-start.19 = (bf16[240,128]{1,0:T(8,128)(2,1)S(1)}, bf16[240,128]{1,0:T(8,128)(2,1)S(1)}, u32[]{:S(2)}, u32[]{:S(2)}) collective-permute-start(bf16[240,128]{1,0:T(8,128)(2,1)S(1)} %add_convert_fusion.2.refs_2_), channel_id=1, source_target_pairs={{0,24},{4,28},{8,0},{12,4},{16,8},{20,12},{24,16},{28,20},{1,25},{... | collective-permute-start | bytes 184328 | tf_op jit(solution)/shard_map/ppermute | solution.py:967
  125.7 2.3 %collective-permute-done.18.refs_4_ = bf16[240,128]{1,0:T(8,128)(2,1)S(1)} collective-permute-done((bf16[240,128]{1,0:T(8,128)(2,1)S(1)}, bf16[240,128]{1,0:T(8,128)(2,1)S(1)}, u32[]{:S(2)}, u32[]{:S(2)}) %collective-permute-start.18) | collective-permute-done | bytes 61472 | tf_op jit(solution)/shard_map/ppermute | solution.py:967
  (55 shorter events, 10.3 us)
Async XLA Ops:
  2.4 4.8 %collective-permute-start = (bf16[64,128]{1,0:T(8,128)(2,1)}, bf16[64,128]{1,0:T(8,128)(2,1)S(1)}, u32[]{:S(2)}, u32[]{:S(2)}) collective-permute-start(bf16[64,128]{1,0:T(8,128)(2,1)} %get-tuple-element.68.refs_0_), channel_id=1, source_target_pairs={{0,1},{1,2},{2,3},{3,0},{4,5},{5,6},{6,7},{7,4},{8,9},{9,10},{10,1... | collective-permute-start | bytes 49160 | tf_op jit(solution)/shard_map/ppermute | solution.py:967
  2.9 5.8 %collective-permute-start.1 = (bf16[64,128]{1,0:T(8,128)(2,1)}, bf16[64,128]{1,0:T(8,128)(2,1)S(1)}, u32[]{:S(2)}, u32[]{:S(2)}) collective-permute-start(bf16[64,128]{1,0:T(8,128)(2,1)} %get-tuple-element.68.refs_0_), channel_id=1, source_target_pairs={{0,2},{1,3},{2,0},{3,1},{4,6},{5,7},{6,4},{7,5},{8,10},{9,11},{10,... | collective-permute-start | bytes 49160 | tf_op jit(solution)/shard_map/ppermute | solution.py:967
  5.4 3.2 %collective-permute-start.2 = (bf16[64,128]{1,0:T(8,128)(2,1)}, bf16[64,128]{1,0:T(8,128)(2,1)S(1)}, u32[]{:S(2)}, u32[]{:S(2)}) collective-permute-start(bf16[64,128]{1,0:T(8,128)(2,1)} %get-tuple-element.68.refs_0_), channel_id=1, source_target_pairs={{0,3},{1,0},{2,1},{3,2},{4,7},{5,4},{6,5},{7,6},{8,11},{9,8},{10,9... | collective-permute-start | bytes 49160 | tf_op jit(solution)/shard_map/ppermute | solution.py:967
  6.9 12.3 %collective-permute-start.3 = (bf16[720,128]{1,0:T(8,128)(2,1)}, bf16[720,128]{1,0:T(8,128)(2,1)S(1)}, u32[]{:S(2)}, u32[]{:S(2)}) collective-permute-start(bf16[720,128]{1,0:T(8,128)(2,1)} %get-tuple-element.70.refs_0_), channel_id=1, source_target_pairs={{0,1},{1,2},{2,3},{3,0},{4,5},{5,6},{6,7},{7,4},{8,9},{9,10},{10,1... | collective-permute-start | bytes 552968 | tf_op jit(solution)/shard_map/ppermute | solution.py:967
  6.9 12.3 %collective-permute-start.4 = (bf16[720,128]{1,0:T(8,128)(2,1)}, bf16[720,128]{1,0:T(8,128)(2,1)S(1)}, u32[]{:S(2)}, u32[]{:S(2)}) collective-permute-start(bf16[720,128]{1,0:T(8,128)(2,1)} %get-tuple-element.70.refs_0_), channel_id=1, source_target_pairs={{0,2},{1,3},{2,0},{3,1},{4,6},{5,7},{6,4},{7,5},{8,10},{9,11},{10,... | collective-permute-start | bytes 552968 | tf_op jit(solution)/shard_map/ppermute | solution.py:967
  7.3 11.9 %collective-permute-start.5 = (bf16[720,128]{1,0:T(8,128)(2,1)}, bf16[720,128]{1,0:T(8,128)(2,1)S(1)}, u32[]{:S(2)}, u32[]{:S(2)}) collective-permute-start(bf16[720,128]{1,0:T(8,128)(2,1)} %get-tuple-element.70.refs_0_), channel_id=1, source_target_pairs={{0,3},{1,0},{2,1},{3,2},{4,7},{5,4},{6,5},{7,6},{8,11},{9,8},{10,9... | collective-permute-start | bytes 552968 | tf_op jit(solution)/shard_map/ppermute | solution.py:967
  8.7 1.4 %copy-start.1 = (bf16[2,3,1024,128]{3,2,1,0:T(8,128)(2,1)S(1)}, bf16[2,3,1024,128]{3,2,1,0:T(8,128)(2,1)}, u32[]{:S(2)}) copy-start(bf16[2,3,1024,128]{3,2,1,0:T(8,128)(2,1)} %param.22) | copy-start | bytes 4718596
  70.0 13.7 %collective-permute-start.8 = (bf16[560,128]{1,0:T(8,128)(2,1)}, bf16[560,128]{1,0:T(8,128)(2,1)S(1)}, u32[]{:S(2)}, u32[]{:S(2)}) collective-permute-start(bf16[560,128]{1,0:T(8,128)(2,1)} %get-tuple-element.93), channel_id=1, source_target_pairs={{0,3},{1,0},{2,1},{3,2},{4,7},{5,4},{6,5},{7,6},{8,11},{9,8},{10,9... | collective-permute-start | bytes 430088 | tf_op jit(solution)/shard_map/ppermute | solution.py:974
  72.1 11.7 %collective-permute-start.7 = (bf16[560,128]{1,0:T(8,128)(2,1)}, bf16[560,128]{1,0:T(8,128)(2,1)S(1)}, u32[]{:S(2)}, u32[]{:S(2)}) collective-permute-start(bf16[560,128]{1,0:T(8,128)(2,1)} %get-tuple-element.92), channel_id=1, source_target_pairs={{0,2},{1,3},{2,0},{3,1},{4,6},{5,7},{6,4},{7,5},{8,10},{9,11},{10,... | collective-permute-start | bytes 430088 | tf_op jit(solution)/shard_map/ppermute | solution.py:974
  72.1 11.7 %collective-permute-start.6 = (bf16[560,128]{1,0:T(8,128)(2,1)}, bf16[560,128]{1,0:T(8,128)(2,1)S(1)}, u32[]{:S(2)}, u32[]{:S(2)}) collective-permute-start(bf16[560,128]{1,0:T(8,128)(2,1)} %get-tuple-element.91), channel_id=1, source_target_pairs={{0,1},{1,2},{2,3},{3,0},{4,5},{5,6},{6,7},{7,4},{8,9},{9,10},{10,1... | collective-permute-start | bytes 430088 | tf_op jit(solution)/shard_map/ppermute | solution.py:974
  72.3 11.5 %copy-start.10 = (bf16[560,128]{1,0:T(8,128)(2,1)S(1)}, bf16[560,128]{1,0:T(8,128)(2,1)}, u32[]{:S(2)}) copy-start(bf16[560,128]{1,0:T(8,128)(2,1)} %get-tuple-element.90) | copy-start | bytes 430084
  83.9 4.7 %copy-start.9 = (bf16[560,128]{1,0:T(8,128)(2,1)}, bf16[560,128]{1,0:T(8,128)(2,1)S(1)}, u32[]{:S(2)}) copy-start(bf16[560,128]{1,0:T(8,128)(2,1)S(1)} %add_convert_fusion.1.refs_4_) | copy-start | bytes 430084
  83.9 16.2 %collective-permute-start.11 = (bf16[560,128]{1,0:T(8,128)(2,1)S(1)}, bf16[560,128]{1,0:T(8,128)(2,1)S(1)}, u32[]{:S(2)}, u32[]{:S(2)}) collective-permute-start(bf16[560,128]{1,0:T(8,128)(2,1)S(1)} %add_convert_fusion.1.refs_4_), channel_id=1, source_target_pairs={{0,24},{4,28},{8,0},{12,4},{16,8},{20,12},{24,16},{28,20},{1,25},{... | collective-permute-start | bytes 430088 | tf_op jit(solution)/shard_map/ppermute | solution.py:967
  87.5 13.2 %collective-permute-start.10 = (bf16[560,128]{1,0:T(8,128)(2,1)S(1)}, bf16[560,128]{1,0:T(8,128)(2,1)S(1)}, u32[]{:S(2)}, u32[]{:S(2)}) collective-permute-start(bf16[560,128]{1,0:T(8,128)(2,1)S(1)} %add_convert_fusion.1.refs_4_), channel_id=1, source_target_pairs={{0,16},{4,20},{8,24},{12,28},{16,0},{20,4},{24,8},{28,12},{1,17},{... | collective-permute-start | bytes 430088 | tf_op jit(solution)/shard_map/ppermute | solution.py:967
  87.5 13.2 %collective-permute-start.9 = (bf16[560,128]{1,0:T(8,128)(2,1)S(1)}, bf16[560,128]{1,0:T(8,128)(2,1)S(1)}, u32[]{:S(2)}, u32[]{:S(2)}) collective-permute-start(bf16[560,128]{1,0:T(8,128)(2,1)S(1)} %add_convert_fusion.1.refs_4_), channel_id=1, source_target_pairs={{0,8},{4,12},{8,16},{12,20},{16,24},{20,28},{24,0},{28,4},{1,9},{5... | collective-permute-start | bytes 430088 | tf_op jit(solution)/shard_map/ppermute | solution.py:967
  102.4 14.2 %copy-start = (bf16[560,128]{1,0:T(8,128)(2,1)S(1)}, bf16[560,128]{1,0:T(8,128)(2,1)}, u32[]{:S(2)}) copy-start(bf16[560,128]{1,0:T(8,128)(2,1)} %add_convert_fusion._after.refs_0_) | copy-start | bytes 430084
  108.1 2.7 %collective-permute-start.15 = (bf16[240,128]{1,0:T(8,128)(2,1)}, bf16[240,128]{1,0:T(8,128)(2,1)S(1)}, u32[]{:S(2)}, u32[]{:S(2)}) collective-permute-start(bf16[240,128]{1,0:T(8,128)(2,1)} %get-tuple-element.103), channel_id=1, source_target_pairs={{0,3},{1,0},{2,1},{3,2},{4,7},{5,4},{6,5},{7,6},{8,11},{9,8},{10,9... | collective-permute-start | bytes 184328 | tf_op jit(solution)/shard_map/ppermute | solution.py:974
  108.5 5.0 %collective-permute-start.14 = (bf16[240,128]{1,0:T(8,128)(2,1)}, bf16[240,128]{1,0:T(8,128)(2,1)S(1)}, u32[]{:S(2)}, u32[]{:S(2)}) collective-permute-start(bf16[240,128]{1,0:T(8,128)(2,1)} %get-tuple-element.102), channel_id=1, source_target_pairs={{0,2},{1,3},{2,0},{3,1},{4,6},{5,7},{6,4},{7,5},{8,10},{9,11},{10,... | collective-permute-start | bytes 184328 | tf_op jit(solution)/shard_map/ppermute | solution.py:974
  110.3 3.9 %collective-permute-start.13 = (bf16[240,128]{1,0:T(8,128)(2,1)}, bf16[240,128]{1,0:T(8,128)(2,1)S(1)}, u32[]{:S(2)}, u32[]{:S(2)}) collective-permute-start(bf16[240,128]{1,0:T(8,128)(2,1)} %get-tuple-element.101), channel_id=1, source_target_pairs={{0,1},{1,2},{2,3},{3,0},{4,5},{5,6},{6,7},{7,4},{8,9},{9,10},{10,1... | collective-permute-start | bytes 184328 | tf_op jit(solution)/shard_map/ppermute | solution.py:974
  115.0 4.6 %collective-permute-start.16 = (bf16[240,128]{1,0:T(8,128)(2,1)S(1)}, bf16[240,128]{1,0:T(8,128)(2,1)S(1)}, u32[]{:S(2)}, u32[]{:S(2)}) collective-permute-start(bf16[240,128]{1,0:T(8,128)(2,1)S(1)} %add_convert_fusion.3), channel_id=1, source_target_pairs={{0,4},{4,0},{8,12},{12,8},{16,20},{20,16},{24,28},{28,24},{1,5},{5... | collective-permute-start | bytes 184328 | tf_op jit(solution)/shard_map/ppermute | solution.py:967
  116.6 8.6 %collective-permute-start.12 = (bf16[560,128]{1,0:T(8,128)(2,1)S(1)}, bf16[560,128]{1,0:T(8,128)(2,1)S(1)}, u32[]{:S(2)}, u32[]{:S(2)}) collective-permute-start(bf16[560,128]{1,0:T(8,128)(2,1)S(1)} %copy-done), channel_id=1, source_target_pairs={{0,4},{4,0},{8,12},{12,8},{16,20},{20,16},{24,28},{28,24},{1,5},{5... | collective-permute-start | bytes 430088 | tf_op jit(solution)/shard_map/ppermute | solution.py:967
  119.6 6.1 %collective-permute-start.17 = (bf16[240,128]{1,0:T(8,128)(2,1)S(1)}, bf16[240,128]{1,0:T(8,128)(2,1)S(1)}, u32[]{:S(2)}, u32[]{:S(2)}) collective-permute-start(bf16[240,128]{1,0:T(8,128)(2,1)S(1)} %add_convert_fusion.2.refs_2_), channel_id=1, source_target_pairs={{0,8},{4,12},{8,16},{12,20},{16,24},{20,28},{24,0},{28,4},{1,9},{5... | collective-permute-start | bytes 184328 | tf_op jit(solution)/shard_map/ppermute | solution.py:967
  122.2 5.9 %collective-permute-start.18 = (bf16[240,128]{1,0:T(8,128)(2,1)S(1)}, bf16[240,128]{1,0:T(8,128)(2,1)S(1)}, u32[]{:S(2)}, u32[]{:S(2)}) collective-permute-start(bf16[240,128]{1,0:T(8,128)(2,1)S(1)} %add_convert_fusion.2.refs_2_), channel_id=1, source_target_pairs={{0,16},{4,20},{8,24},{12,28},{16,0},{20,4},{24,8},{28,12},{1,17},{... | collective-permute-start | bytes 184328 | tf_op jit(solution)/shard_map/ppermute | solution.py:967
  123.3 4.7 %collective-permute-start.19 = (bf16[240,128]{1,0:T(8,128)(2,1)S(1)}, bf16[240,128]{1,0:T(8,128)(2,1)S(1)}, u32[]{:S(2)}, u32[]{:S(2)}) collective-permute-start(bf16[240,128]{1,0:T(8,128)(2,1)S(1)} %add_convert_fusion.2.refs_2_), channel_id=1, source_target_pairs={{0,24},{4,28},{8,0},{12,4},{16,8},{20,12},{24,16},{28,20},{1,25},{... | collective-permute-start | bytes 184328 | tf_op jit(solution)/shard_map/ppermute | solution.py:967
  (10 other events, 8.0 us)

commit v2 on v0

--- a/solution.py
+++ b/solution.py
@@ -1365,6 +1365,7 @@
             pltpu.VMEM((main_rows, width), f32),
             pltpu.VMEM((rest_rows, width), f32),
         ],
+        compiler_params=pltpu.CompilerParams(vmem_limit_bytes=VMEM // 8),
         name="unpack",
     )(*main_parts, *parts)
     outs = [out.reshape(piece) if out.shape == (1, piece) else out for out in outs]

time: 128 us -> 126 us (0.984)
  no operation moved by 1% of the time
where the time goes in v2:
time: 126 us
  Pallas kernels  85.7 us (68%)
  starting transfers between devices  23.5 us (19%)
  waiting for transfers between devices  11.8 us (9%)
  other arithmetic  2.64 us (2%)
  local copies, waits for them, and re-layouts  1.28 us (1%)
    pallas_call x1, Pallas kernels, shards_fn(): pl.pallas_call(partial(main_kernel, funcs=funcs, experts=experts, shards=...  49.5 us
    pallas_call x2, Pallas kernels, rest_call(): pl.pallas_call(partial(rest_kernel, funcs=funcs, item=item, first_call=fi...  22.9 us
    ppermute x14, starting transfers between devices, spread(): lax.ppermute(value, axis, route(size, shift, digit, stride))  18.7 us
    ppermute x14, waiting for transfers between devices, spread(): lax.ppermute(value, axis, route(size, shift, digit, stride))  7.37 us
    pallas_call x1, Pallas kernels, shards_fn(): pl.pallas_call(partial(points_back, shards=shards), grid=(items,), in_spe...  5.73 us
    pallas_call x1, Pallas kernels, shards_fn(): pl.pallas_call(partial(points_forward, funcs=funcs, shards=shards), grid=...  4.91 us
    ppermute x6, starting transfers between devices, exchange(): lax.ppermute(values[shift], axis, route(size, shift, digit, stride))  4.82 us
    ppermute x6, waiting for transfers between devices, exchange(): lax.ppermute(values[shift], axis, route(size, shift, digit, stride))  4.38 us
  transfers between devices with their start and end apart: 20, of which 10 were waited for; matrix products, arithmetic and copies ran while one was open for 0% of the time, Pallas kernels for 22%

profile of v2, /device:TPU:0, one launch (start us, length us, event | category | flops | bytes accessed | tf_op | source)
XLA Modules:
  0.0 125.8 jit_solution(7251368936078023587)
XLA Ops:
  0.7 1.8 %pack.1 = (bf16[64,128]{1,0:T(8,128)(2,1)}, bf16[720,128]{1,0:T(8,128)(2,1)}) custom-call(bf16[32,128]{1,0:T(8,128)(2,1)} %refs_0_.1, bf16[32,128]{1,0:T(8,128)(2,1)} %refs_1_.1, bf16[32,128]{1,0:T(8,128)(2,1)} %refs_2_.1, bf16[32,128]{1,0:T(8,128)(2,1)} %refs_3_.1, bf16[32,128]{1,0:T(8,128)(2,1)} %refs_4_.1, bf16[32,128]{1,0:T(8,128)(2,1)} %refs_5_.1, ...), custom_call_target="tpu_custom_call" | custom-call | tf_op jit(solution)/shard_map/pack/pallas_call | solution.py:1046
  2.9 2.6 %collective-permute-start.1 = (bf16[64,128]{1,0:T(8,128)(2,1)}, bf16[64,128]{1,0:T(8,128)(2,1)S(1)}, u32[]{:S(2)}, u32[]{:S(2)}) collective-permute-start(bf16[64,128]{1,0:T(8,128)(2,1)} %get-tuple-element.68.refs_0_), channel_id=1, source_target_pairs={{0,2},{1,3},{2,0},{3,1},{4,6},{5,7},{6,4},{7,5},{8,10},{9,11},{10,... | collective-permute-start | bytes 49160 | tf_op jit(solution)/shard_map/ppermute | solution.py:967
  5.4 1.4 %collective-permute-start.2 = (bf16[64,128]{1,0:T(8,128)(2,1)}, bf16[64,128]{1,0:T(8,128)(2,1)S(1)}, u32[]{:S(2)}, u32[]{:S(2)}) collective-permute-start(bf16[64,128]{1,0:T(8,128)(2,1)} %get-tuple-element.68.refs_0_), channel_id=1, source_target_pairs={{0,3},{1,0},{2,1},{3,2},{4,7},{5,4},{6,5},{7,6},{8,11},{9,8},{10,9... | collective-permute-start | bytes 49160 | tf_op jit(solution)/shard_map/ppermute | solution.py:967
  7.3 1.4 %collective-permute-start.5 = (bf16[720,128]{1,0:T(8,128)(2,1)}, bf16[720,128]{1,0:T(8,128)(2,1)S(1)}, u32[]{:S(2)}, u32[]{:S(2)}) collective-permute-start(bf16[720,128]{1,0:T(8,128)(2,1)} %get-tuple-element.70.refs_0_), channel_id=1, source_target_pairs={{0,3},{1,0},{2,1},{3,2},{4,7},{5,4},{6,5},{7,6},{8,11},{9,8},{10,9... | collective-permute-start | bytes 552968 | tf_op jit(solution)/shard_map/ppermute | solution.py:967
  9.3 4.9 %points_forward.1 = (bf16[2,416,128]{2,1,0:T(8,128)(2,1)}, bf16[2,128,512]{2,1,0:T(8,128)(2,1)}, bf16[6,128,1024]{2,1,0:T(8,128)(2,1)}, bf16[6,128,1024]{2,1,0:T(8,128)(2,1)}) custom-call(s32[2,3]{1,0:T(2,128)} %counts.1, s32[2,3]{1,0:T(2,128)} %presence.5, bf16[6,1024,128]{2,1,0:T(8,128)(2,1)} %bitcast.14, bf16[64,128]{1,0:T(8,128)(2,1)} %get-tuple-element.68.refs_0_, ...), custom_call_target="tpu_custom_call" | custom-call | flops 8000000000 | bytes 1000000 | tf_op jit(solution)/shard_map/points_forward/pallas_call | solution.py:1079
  14.6 1.5 %collective-permute-done.5.refs_3_ = bf16[720,128]{1,0:T(8,128)(2,1)S(1)} collective-permute-done((bf16[720,128]{1,0:T(8,128)(2,1)}, bf16[720,128]{1,0:T(8,128)(2,1)S(1)}, u32[]{:S(2)}, u32[]{:S(2)}) %collective-permute-start.5) | collective-permute-done | bytes 184352 | tf_op jit(solution)/shard_map/ppermute | solution.py:967
  16.7 49.5 %main.1 = (bf16[8192,128]{1,0:T(8,128)(2,1)}, bf16[128,8192]{1,0:T(8,128)(2,1)}, bf16[128,8192]{1,0:T(8,128)(2,1)}, bf16[128,8192]{1,0:T(8,128)(2,1)}, bf16[128,...) custom-call(bf16[8192,128]{1,0:T(8,128)(2,1)} %tokens.1, ...), custom_call_target="tpu_custom_call" | custom-call | flops 80000000000 | bytes 1000000 | tf_op jit(solution)/shard_map/main/pallas_call | solution.py:1133
  66.3 1.9 %collective-permute-start.8 = (bf16[560,128]{1,0:T(8,128)(2,1)}, bf16[560,128]{1,0:T(8,128)(2,1)S(1)}, u32[]{:S(2)}, u32[]{:S(2)}) collective-permute-start(bf16[560,128]{1,0:T(8,128)(2,1)} %get-tuple-element.93), channel_id=1, source_target_pairs={{0,3},{1,0},{2,1},{3,2},{4,7},{5,4},{6,5},{7,6},{8,11},{9,8},{10,9... | collective-permute-start | bytes 430088 | tf_op jit(solution)/shard_map/ppermute | solution.py:974
  68.2 1.5 %collective-permute-start.7 = (bf16[560,128]{1,0:T(8,128)(2,1)}, bf16[560,128]{1,0:T(8,128)(2,1)S(1)}, u32[]{:S(2)}, u32[]{:S(2)}) collective-permute-start(bf16[560,128]{1,0:T(8,128)(2,1)} %get-tuple-element.92), channel_id=1, source_target_pairs={{0,2},{1,3},{2,0},{3,1},{4,6},{5,7},{6,4},{7,5},{8,10},{9,11},{10,... | collective-permute-start | bytes 430088 | tf_op jit(solution)/shard_map/ppermute | solution.py:974
  69.7 11.4 %rest.2 = (f32[8192,128]{1,0:T(8,128)}, bf16[6,128,128]{2,1,0:T(8,128)(2,1)}, f32[6,128,128]{2,1,0:T(8,128)}, f32[896,128]{1,0:T(8,128)}) custom-call(s32[2,3]{1,0:T(2,128)} %presence.5, bf16[128,8192]{1,0:T(8,128)(2,1)} %get-tuple-element.72.hat_in, f32[8,8192]{1,0:T(8,128)} %get-tuple-element.73.scale_in, bf16[128,8192]{1,0:T(8,128)(2,1)} %get-tuple-element.74.normed_in, ...), custom_call_target="tpu_custom_call" | custom-call | flops 17999998976 | bytes 1000000 | tf_op jit(solution)/shard_map/rest/pallas_call | solution.py:1273
  81.2 3.6 %collective-permute-start.11 = (bf16[560,128]{1,0:T(8,128)(2,1)S(1)}, bf16[560,128]{1,0:T(8,128)(2,1)S(1)}, u32[]{:S(2)}, u32[]{:S(2)}) collective-permute-start(bf16[560,128]{1,0:T(8,128)(2,1)S(1)} %add_convert_fusion.1.refs_4_), channel_id=1, source_target_pairs={{0,24},{4,28},{8,0},{12,4},{16,8},{20,12},{24,16},{28,20},{1,25},{... | collective-permute-start | bytes 430088 | tf_op jit(solution)/shard_map/ppermute | solution.py:967
  84.9 1.0 collective-permute-start.9
  85.9 11.5 %rest.3 = (f32[8192,128]{1,0:T(8,128)}, bf16[6,128,128]{2,1,0:T(8,128)(2,1)}, f32[6,128,128]{2,1,0:T(8,128)}, f32[896,128]{1,0:T(8,128)}) custom-call(s32[2,3]{1,0:T(2,128)} %presence.5, bf16[128,8192]{1,0:T(8,128)(2,1)} %get-tuple-element.72.hat_in, ...), custom_call_target="tpu_custom_call", output_to_operand_aliasing={{0}: (16, {}), {1}: (17, {}), {2}: (18, {})} | custom-call | flops 17999998976 | bytes 1000000 | tf_op jit(solution)/shard_map/rest/pallas_call | solution.py:1273
  98.1 1.7 %add_convert_fusion._after.refs_0_ = bf16[560,128]{1,0:T(8,128)(2,1)} fusion(bf16[560,128]{1,0:T(8,128)(2,1)S(1)} %collective-permute-done.11, bf16[560,128]{1,0:T(8,128)(2,1)S(1)} %collective-permute-done.10, bf16[560,128]{1,0:T(8,128)(2,1)S(1)} %collective-permute-done.9, bf16[560,128]{1,0:T(8,128)(2,1)} %copy-done.1), kind=kLoop, calls=%fused_computation | loop fusion | flops 573440 | bytes 716800 | tf_op jit(solution)/shard_map/convert_element_type | solution.py:991
  99.8 5.7 %points_back.1 = (bf16[240,128]{1,0:T(8,128)(2,1)}, bf16[240,128]{1,0:T(8,128)(2,1)}, bf16[240,128]{1,0:T(8,128)(2,1)}, bf16[240,128]{1,0:T(8,128)(2,1)}) custom-call(bf16[6,1024,128]{2,1,0:T(8,128)(2,1)} %bitcast.15, bf16[6,128,1024]{2,1,0:T(8,128)(2,1)} %get-tuple-element.95.keys_in, bf16[6,128,1024]{2,1,0:T(8,128)(2,1)} %get-tuple-element.96.values_in, ...), custom_call_target="tpu_custom_call" | custom-call | flops 7000000000 | bytes 1000000 | tf_op jit(solution)/shard_map/points_back/pallas_call | solution.py:1313
  107.0 1.8 %collective-permute-done.15 = bf16[240,128]{1,0:T(8,128)(2,1)S(1)} collective-permute-done((bf16[240,128]{1,0:T(8,128)(2,1)}, bf16[240,128]{1,0:T(8,128)(2,1)S(1)}, u32[]{:S(2)}, u32[]{:S(2)}) %collective-permute-start.15) | collective-permute-done | bytes 61472 | tf_op jit(solution)/shard_map/ppermute | solution.py:974
  108.8 2.4 %collective-permute-done.14 = bf16[240,128]{1,0:T(8,128)(2,1)S(1)} collective-permute-done((bf16[240,128]{1,0:T(8,128)(2,1)}, bf16[240,128]{1,0:T(8,128)(2,1)S(1)}, u32[]{:S(2)}, u32[]{:S(2)}) %collective-permute-start.14) | collective-permute-done | bytes 61472 | tf_op jit(solution)/shard_map/ppermute | solution.py:974
  111.3 0.9 add_convert_fusion.3
  112.2 1.5 %collective-permute-start.16 = (bf16[240,128]{1,0:T(8,128)(2,1)S(1)}, bf16[240,128]{1,0:T(8,128)(2,1)S(1)}, u32[]{:S(2)}, u32[]{:S(2)}) collective-permute-start(bf16[240,128]{1,0:T(8,128)(2,1)S(1)} %add_convert_fusion.3), channel_id=1, source_target_pairs={{0,4},{4,0},{8,12},{12,8},{16,20},{20,16},{24,28},{28,24},{1,5},{5... | collective-permute-start | bytes 184328 | tf_op jit(solution)/shard_map/ppermute | solution.py:967
  114.3 2.8 %collective-permute-done.16 = bf16[240,128]{1,0:T(8,128)(2,1)S(1)} collective-permute-done((bf16[240,128]{1,0:T(8,128)(2,1)S(1)}, bf16[240,128]{1,0:T(8,128)(2,1)S(1)}, u32[]{:S(2)}, u32[]{:S(2)}) %collective-permute-start.16) | collective-permute-done | bytes 61472 | tf_op jit(solution)/shard_map/ppermute | solution.py:967
  117.1 1.9 %collective-permute-start.17 = (bf16[240,128]{1,0:T(8,128)(2,1)S(1)}, bf16[240,128]{1,0:T(8,128)(2,1)S(1)}, u32[]{:S(2)}, u32[]{:S(2)}) collective-permute-start(bf16[240,128]{1,0:T(8,128)(2,1)S(1)} %add_convert_fusion.2.refs_2_), channel_id=1, source_target_pairs={{0,8},{4,12},{8,16},{12,20},{16,24},{20,28},{24,0},{28,4},{1,9},{5... | collective-permute-start | bytes 184328 | tf_op jit(solution)/shard_map/ppermute | solution.py:967
  119.0 1.2 collective-permute-start.18
  120.2 2.6 %collective-permute-start.19 = (bf16[240,128]{1,0:T(8,128)(2,1)S(1)}, bf16[240,128]{1,0:T(8,128)(2,1)S(1)}, u32[]{:S(2)}, u32[]{:S(2)}) collective-permute-start(bf16[240,128]{1,0:T(8,128)(2,1)S(1)} %add_convert_fusion.2.refs_2_), channel_id=1, source_target_pairs={{0,24},{4,28},{8,0},{12,4},{16,8},{20,12},{24,16},{28,20},{1,25},{... | collective-permute-start | bytes 184328 | tf_op jit(solution)/shard_map/ppermute | solution.py:967
  123.2 1.0 collective-permute-done.18.refs_4_
  (45 shorter events, 7.2 us)
Async XLA Ops:
  2.4 4.8 %collective-permute-start = (bf16[64,128]{1,0:T(8,128)(2,1)}, bf16[64,128]{1,0:T(8,128)(2,1)S(1)}, u32[]{:S(2)}, u32[]{:S(2)}) collective-permute-start(bf16[64,128]{1,0:T(8,128)(2,1)} %get-tuple-element.68.refs_0_), channel_id=1, source_target_pairs={{0,1},{1,2},{2,3},{3,0},{4,5},{5,6},{6,7},{7,4},{8,9},{9,10},{10,1... | collective-permute-start | bytes 49160 | tf_op jit(solution)/shard_map/ppermute | solution.py:967
  2.9 5.8 %collective-permute-start.1 = (bf16[64,128]{1,0:T(8,128)(2,1)}, bf16[64,128]{1,0:T(8,128)(2,1)S(1)}, u32[]{:S(2)}, u32[]{:S(2)}) collective-permute-start(bf16[64,128]{1,0:T(8,128)(2,1)} %get-tuple-element.68.refs_0_), channel_id=1, source_target_pairs={{0,2},{1,3},{2,0},{3,1},{4,6},{5,7},{6,4},{7,5},{8,10},{9,11},{10,... | collective-permute-start | bytes 49160 | tf_op jit(solution)/shard_map/ppermute | solution.py:967
  5.4 3.2 %collective-permute-start.2 = (bf16[64,128]{1,0:T(8,128)(2,1)}, bf16[64,128]{1,0:T(8,128)(2,1)S(1)}, u32[]{:S(2)}, u32[]{:S(2)}) collective-permute-start(bf16[64,128]{1,0:T(8,128)(2,1)} %get-tuple-element.68.refs_0_), channel_id=1, source_target_pairs={{0,3},{1,0},{2,1},{3,2},{4,7},{5,4},{6,5},{7,6},{8,11},{9,8},{10,9... | collective-permute-start | bytes 49160 | tf_op jit(solution)/shard_map/ppermute | solution.py:967
  6.9 7.3 %collective-permute-start.3 = (bf16[720,128]{1,0:T(8,128)(2,1)}, bf16[720,128]{1,0:T(8,128)(2,1)S(1)}, u32[]{:S(2)}, u32[]{:S(2)}) collective-permute-start(bf16[720,128]{1,0:T(8,128)(2,1)} %get-tuple-element.70.refs_0_), channel_id=1, source_target_pairs={{0,1},{1,2},{2,3},{3,0},{4,5},{5,6},{6,7},{7,4},{8,9},{9,10},{10,1... | collective-permute-start | bytes 552968 | tf_op jit(solution)/shard_map/ppermute | solution.py:967
  6.9 7.7 %collective-permute-start.4 = (bf16[720,128]{1,0:T(8,128)(2,1)}, bf16[720,128]{1,0:T(8,128)(2,1)S(1)}, u32[]{:S(2)}, u32[]{:S(2)}) collective-permute-start(bf16[720,128]{1,0:T(8,128)(2,1)} %get-tuple-element.70.refs_0_), channel_id=1, source_target_pairs={{0,2},{1,3},{2,0},{3,1},{4,6},{5,7},{6,4},{7,5},{8,10},{9,11},{10,... | collective-permute-start | bytes 552968 | tf_op jit(solution)/shard_map/ppermute | solution.py:967
  7.3 8.8 %collective-permute-start.5 = (bf16[720,128]{1,0:T(8,128)(2,1)}, bf16[720,128]{1,0:T(8,128)(2,1)S(1)}, u32[]{:S(2)}, u32[]{:S(2)}) collective-permute-start(bf16[720,128]{1,0:T(8,128)(2,1)} %get-tuple-element.70.refs_0_), channel_id=1, source_target_pairs={{0,3},{1,0},{2,1},{3,2},{4,7},{5,4},{6,5},{7,6},{8,11},{9,8},{10,9... | collective-permute-start | bytes 552968 | tf_op jit(solution)/shard_map/ppermute | solution.py:967
  14.2 1.9 %copy-start.3 = (bf16[720,128]{1,0:T(8,128)(2,1)}, bf16[720,128]{1,0:T(8,128)(2,1)S(1)}, u32[]{:S(2)}) copy-start(bf16[720,128]{1,0:T(8,128)(2,1)S(1)} %collective-permute-done.3.refs_1_) | copy-start | bytes 552964
  66.3 14.8 %collective-permute-start.8 = (bf16[560,128]{1,0:T(8,128)(2,1)}, bf16[560,128]{1,0:T(8,128)(2,1)S(1)}, u32[]{:S(2)}, u32[]{:S(2)}) collective-permute-start(bf16[560,128]{1,0:T(8,128)(2,1)} %get-tuple-element.93), channel_id=1, source_target_pairs={{0,3},{1,0},{2,1},{3,2},{4,7},{5,4},{6,5},{7,6},{8,11},{9,8},{10,9... | collective-permute-start | bytes 430088 | tf_op jit(solution)/shard_map/ppermute | solution.py:974
  68.2 13.0 %collective-permute-start.7 = (bf16[560,128]{1,0:T(8,128)(2,1)}, bf16[560,128]{1,0:T(8,128)(2,1)S(1)}, u32[]{:S(2)}, u32[]{:S(2)}) collective-permute-start(bf16[560,128]{1,0:T(8,128)(2,1)} %get-tuple-element.92), channel_id=1, source_target_pairs={{0,2},{1,3},{2,0},{3,1},{4,6},{5,7},{6,4},{7,5},{8,10},{9,11},{10,... | collective-permute-start | bytes 430088 | tf_op jit(solution)/shard_map/ppermute | solution.py:974
  69.7 11.4 %collective-permute-start.6 = (bf16[560,128]{1,0:T(8,128)(2,1)}, bf16[560,128]{1,0:T(8,128)(2,1)S(1)}, u32[]{:S(2)}, u32[]{:S(2)}) collective-permute-start(bf16[560,128]{1,0:T(8,128)(2,1)} %get-tuple-element.91), channel_id=1, source_target_pairs={{0,1},{1,2},{2,3},{3,0},{4,5},{5,6},{6,7},{7,4},{8,9},{9,10},{10,1... | collective-permute-start | bytes 430088 | tf_op jit(solution)/shard_map/ppermute | solution.py:974
  69.7 11.5 %copy-start.2 = (bf16[560,128]{1,0:T(8,128)(2,1)S(1)}, bf16[560,128]{1,0:T(8,128)(2,1)}, u32[]{:S(2)}) copy-start(bf16[560,128]{1,0:T(8,128)(2,1)} %get-tuple-element.90) | copy-start | bytes 430084
  81.2 4.7 %copy-start.1 = (bf16[560,128]{1,0:T(8,128)(2,1)}, bf16[560,128]{1,0:T(8,128)(2,1)S(1)}, u32[]{:S(2)}) copy-start(bf16[560,128]{1,0:T(8,128)(2,1)S(1)} %add_convert_fusion.1.refs_4_) | copy-start | bytes 430084
  81.2 16.2 %collective-permute-start.11 = (bf16[560,128]{1,0:T(8,128)(2,1)S(1)}, bf16[560,128]{1,0:T(8,128)(2,1)S(1)}, u32[]{:S(2)}, u32[]{:S(2)}) collective-permute-start(bf16[560,128]{1,0:T(8,128)(2,1)S(1)} %add_convert_fusion.1.refs_4_), channel_id=1, source_target_pairs={{0,24},{4,28},{8,0},{12,4},{16,8},{20,12},{24,16},{28,20},{1,25},{... | collective-permute-start | bytes 430088 | tf_op jit(solution)/shard_map/ppermute | solution.py:967
  84.9 13.3 %collective-permute-start.10 = (bf16[560,128]{1,0:T(8,128)(2,1)S(1)}, bf16[560,128]{1,0:T(8,128)(2,1)S(1)}, u32[]{:S(2)}, u32[]{:S(2)}) collective-permute-start(bf16[560,128]{1,0:T(8,128)(2,1)S(1)} %add_convert_fusion.1.refs_4_), channel_id=1, source_target_pairs={{0,16},{4,20},{8,24},{12,28},{16,0},{20,4},{24,8},{28,12},{1,17},{... | collective-permute-start | bytes 430088 | tf_op jit(solution)/shard_map/ppermute | solution.py:967
  84.9 13.3 %collective-permute-start.9 = (bf16[560,128]{1,0:T(8,128)(2,1)S(1)}, bf16[560,128]{1,0:T(8,128)(2,1)S(1)}, u32[]{:S(2)}, u32[]{:S(2)}) collective-permute-start(bf16[560,128]{1,0:T(8,128)(2,1)S(1)} %add_convert_fusion.1.refs_4_), channel_id=1, source_target_pairs={{0,8},{4,12},{8,16},{12,20},{16,24},{20,28},{24,0},{28,4},{1,9},{5... | collective-permute-start | bytes 430088 | tf_op jit(solution)/shard_map/ppermute | solution.py:967
  99.8 13.9 %copy-start = (bf16[560,128]{1,0:T(8,128)(2,1)S(1)}, bf16[560,128]{1,0:T(8,128)(2,1)}, u32[]{:S(2)}) copy-start(bf16[560,128]{1,0:T(8,128)(2,1)} %add_convert_fusion._after.refs_0_) | copy-start | bytes 430084
  105.5 3.2 %collective-permute-start.15 = (bf16[240,128]{1,0:T(8,128)(2,1)}, bf16[240,128]{1,0:T(8,128)(2,1)S(1)}, u32[]{:S(2)}, u32[]{:S(2)}) collective-permute-start(bf16[240,128]{1,0:T(8,128)(2,1)} %get-tuple-element.103), channel_id=1, source_target_pairs={{0,3},{1,0},{2,1},{3,2},{4,7},{5,4},{6,5},{7,6},{8,11},{9,8},{10,9... | collective-permute-start | bytes 184328 | tf_op jit(solution)/shard_map/ppermute | solution.py:974
  106.2 5.0 %collective-permute-start.14 = (bf16[240,128]{1,0:T(8,128)(2,1)}, bf16[240,128]{1,0:T(8,128)(2,1)S(1)}, u32[]{:S(2)}, u32[]{:S(2)}) collective-permute-start(bf16[240,128]{1,0:T(8,128)(2,1)} %get-tuple-element.102), channel_id=1, source_target_pairs={{0,2},{1,3},{2,0},{3,1},{4,6},{5,7},{6,4},{7,5},{8,10},{9,11},{10,... | collective-permute-start | bytes 184328 | tf_op jit(solution)/shard_map/ppermute | solution.py:974
  107.0 4.4 %collective-permute-start.13 = (bf16[240,128]{1,0:T(8,128)(2,1)}, bf16[240,128]{1,0:T(8,128)(2,1)S(1)}, u32[]{:S(2)}, u32[]{:S(2)}) collective-permute-start(bf16[240,128]{1,0:T(8,128)(2,1)} %get-tuple-element.101), channel_id=1, source_target_pairs={{0,1},{1,2},{2,3},{3,0},{4,5},{5,6},{6,7},{7,4},{8,9},{9,10},{10,1... | collective-permute-start | bytes 184328 | tf_op jit(solution)/shard_map/ppermute | solution.py:974
  112.2 4.9 %collective-permute-start.16 = (bf16[240,128]{1,0:T(8,128)(2,1)S(1)}, bf16[240,128]{1,0:T(8,128)(2,1)S(1)}, u32[]{:S(2)}, u32[]{:S(2)}) collective-permute-start(bf16[240,128]{1,0:T(8,128)(2,1)S(1)} %add_convert_fusion.3), channel_id=1, source_target_pairs={{0,4},{4,0},{8,12},{12,8},{16,20},{20,16},{24,28},{28,24},{1,5},{5... | collective-permute-start | bytes 184328 | tf_op jit(solution)/shard_map/ppermute | solution.py:967
  113.7 9.1 %collective-permute-start.12 = (bf16[560,128]{1,0:T(8,128)(2,1)S(1)}, bf16[560,128]{1,0:T(8,128)(2,1)S(1)}, u32[]{:S(2)}, u32[]{:S(2)}) collective-permute-start(bf16[560,128]{1,0:T(8,128)(2,1)S(1)} %copy-done), channel_id=1, source_target_pairs={{0,4},{4,0},{8,12},{12,8},{16,20},{20,16},{24,28},{28,24},{1,5},{5... | collective-permute-start | bytes 430088 | tf_op jit(solution)/shard_map/ppermute | solution.py:967
  117.1 6.1 %collective-permute-start.17 = (bf16[240,128]{1,0:T(8,128)(2,1)S(1)}, bf16[240,128]{1,0:T(8,128)(2,1)S(1)}, u32[]{:S(2)}, u32[]{:S(2)}) collective-permute-start(bf16[240,128]{1,0:T(8,128)(2,1)S(1)} %add_convert_fusion.2.refs_2_), channel_id=1, source_target_pairs={{0,8},{4,12},{8,16},{12,20},{16,24},{20,28},{24,0},{28,4},{1,9},{5... | collective-permute-start | bytes 184328 | tf_op jit(solution)/shard_map/ppermute | solution.py:967
  119.0 5.2 %collective-permute-start.18 = (bf16[240,128]{1,0:T(8,128)(2,1)S(1)}, bf16[240,128]{1,0:T(8,128)(2,1)S(1)}, u32[]{:S(2)}, u32[]{:S(2)}) collective-permute-start(bf16[240,128]{1,0:T(8,128)(2,1)S(1)} %add_convert_fusion.2.refs_2_), channel_id=1, source_target_pairs={{0,16},{4,20},{8,24},{12,28},{16,0},{20,4},{24,8},{28,12},{1,17},{... | collective-permute-start | bytes 184328 | tf_op jit(solution)/shard_map/ppermute | solution.py:967
  120.2 4.6 %collective-permute-start.19 = (bf16[240,128]{1,0:T(8,128)(2,1)S(1)}, bf16[240,128]{1,0:T(8,128)(2,1)S(1)}, u32[]{:S(2)}, u32[]{:S(2)}) collective-permute-start(bf16[240,128]{1,0:T(8,128)(2,1)S(1)} %add_convert_fusion.2.refs_2_), channel_id=1, source_target_pairs={{0,24},{4,28},{8,0},{12,4},{16,8},{20,12},{24,16},{28,20},{1,25},{... | collective-permute-start | bytes 184328 | tf_op jit(solution)/shard_map/ppermute | solution.py:967
  (5 other events, 4.8 us)
